TPU v7x, 32 devices: a whole 2x2x4 slice. The times are simulated.
32 devices in a mesh: ctx: 8 (over z, y), kvh: 4 (over x, core).
Axes of the slice: x: 2, y: 2, z: 4, core: 2. Of those that a mesh axis runs over, the one named last changes fastest.
Arguments:
- queries: bfloat16 [1024, 32, 128], P('ctx', 'kvh'), may hold values from -32 to 32
- new_keys: bfloat16 [1024, 8, 128], P('ctx', 'kvh'), may hold values from -6 to 6
- new_values: bfloat16 [1024, 8, 128], P('ctx', 'kvh'), may hold values from -6 to 6
- cache_keys: bfloat16 [65536, 8, 128], P('ctx', 'kvh'), may hold values from -6 to 6
- cache_values: bfloat16 [65536, 8, 128], P('ctx', 'kvh'), may hold values from -6 to 6
- verticals: int32 [32, 16], P('kvh'), may hold values from 0 to 1023, as said below
- offsets: int32 [32, 96], P('kvh'), may hold values from 0 to 255, as said below
- out_weight: bfloat16 [4096, 4096], P('kvh'), may hold values from -0.09375 to 0.09375
Outputs:
- output: bfloat16 [1024, 4096], P(('ctx', 'kvh'))
Inputs may be any that keep to these rules, and one draw needn't show every extreme that they name: `verticals`: 16 distinct cache blocks per head; at most 2 of one head's lie among the 128 blocks of one index of ctx, and exactly 2 do for some index, for every head. 96 distinct offsets per head; the first is 0 and the second is 255.
All inputs are finite; a program needn't handle non-finite values.
Results may differ from a plain program's by a relative error of at most 0.015.
Values may be sent and summed in bfloat16 or wider, within the bound.
A program may use at most 256 MiB of HBM per device.

v0:
```python
import math

import jax
import jax.numpy as jnp
from jax import lax
from jax.sharding import PartitionSpec as P

BLOCK = 64
SPAN = 256
VCAP = 2


lowest_score = -1e30


def from_root(block, axis, owner):
    block = jnp.where(lax.axis_index(axis) == owner, block, jnp.zeros_like(block))
    return lax.psum(block, axis)


def softmax_part(scores, allowed, values, form):
    masked = jnp.where(allowed, scores, lowest_score)
    maximum = jnp.max(masked, axis=-1)
    weights = jnp.where(allowed, jnp.exp(masked - maximum[..., None]), 0.0)
    totals = jnp.sum(weights, axis=-1)
    summed = jnp.einsum(
        form, weights.astype(jnp.bfloat16), values, preferred_element_type=jnp.float32
    )
    return (maximum, totals, summed)


def merge_pair(first_part, second):
    maximum = jnp.maximum(first_part[0], second[0])
    factor_one = jnp.exp(first_part[0] - maximum)
    factor_two = jnp.exp(second[0] - maximum)
    totals = first_part[1] * factor_one + second[1] * factor_two
    summed = first_part[2] * factor_one[..., None] + second[2] * factor_two[..., None]
    return (maximum, totals, summed)


def local_slots(verticals, lower_block, blocks_dev):
    inside = (verticals >= lower_block) & (verticals < lower_block + blocks_dev)
    counts = inside.astype(jnp.int32)
    slot_rank = jnp.cumsum(counts, axis=1) - counts
    slot_ids = jnp.arange(VCAP, dtype=jnp.int32)
    onehot = (inside[:, None, :] & (slot_rank[:, None, :] == slot_ids[None, :, None])).astype(
        jnp.int32
    )
    filled = jnp.sum(onehot, axis=2) > 0
    global_block = jnp.where(filled, jnp.sum(onehot * verticals[:, None, :], axis=2), -1)
    local_block = jnp.where(filled, global_block - lower_block, 0)
    return (global_block, local_block)


def vertical_part(
    row_data, block_ids, slot_keys, slot_values, global_block, offsets, cache_blocks, scaling
):
    head_count, slot_count = global_block.shape
    head_width = slot_keys.shape[-1]
    block_count = block_ids.shape[0]
    flat_keys = slot_keys.reshape(head_count, slot_count * BLOCK, head_width)
    flat_values = slot_values.reshape(head_count, slot_count * BLOCK, head_width)
    scores = (
        jnp.einsum("tjd,jkd->tjk", row_data, flat_keys, preferred_element_type=jnp.float32)
        * scaling
    )
    slash_blocks = cache_blocks + block_ids[:, None, None] - offsets[None, :, :]
    repeated = jnp.any(global_block[None, :, :, None] == slash_blocks[:, :, None, :], axis=-1)
    usable = (global_block[None] >= 0) & jnp.logical_not(repeated)
    allowed = jnp.broadcast_to(
        usable[:, None, :, :, None], (block_count, BLOCK, head_count, slot_count, BLOCK)
    )
    allowed = allowed.reshape(block_count * BLOCK, head_count, slot_count * BLOCK)
    return softmax_part(scores, allowed, flat_values, "tjk,jkd->tjd")


def slash_part(row_data, block_ids, recent_keys, recent_values, offsets, scaling):
    block_count = block_ids.shape[0]
    head_count, diagonals = offsets.shape
    head_width = row_data.shape[-1]
    kv_heads = recent_keys.shape[1]
    key_blocks = recent_keys.reshape(-1, BLOCK, kv_heads, head_width)
    value_blocks = recent_values.reshape(-1, BLOCK, kv_heads, head_width)
    where_block = SPAN + block_ids[:, None, None] - offsets[None, :, :]
    kv_index = (jnp.arange(head_count, dtype=jnp.int32) // (head_count // kv_heads))[None, :, None]
    key_data = key_blocks[where_block, :, kv_index, :]
    value_data = value_blocks[where_block, :, kv_index, :]
    grouped = row_data.reshape(block_count, BLOCK, head_count, head_width)
    scores = (
        jnp.einsum("brjd,bjskd->brjsk", grouped, key_data, preferred_element_type=jnp.float32)
        * scaling
    )
    row_pos = jnp.arange(BLOCK, dtype=jnp.int32)[:, None, None, None]
    key_pos = jnp.arange(BLOCK, dtype=jnp.int32)[None, None, None, :]
    visible = (offsets[None, :, :, None] != 0) | (key_pos <= row_pos)
    allowed = jnp.broadcast_to(visible[None], (block_count, BLOCK, head_count, diagonals, BLOCK))
    allowed = allowed.reshape(block_count, BLOCK, head_count, diagonals * BLOCK)
    maximum, totals, summed = softmax_part(
        scores.reshape(block_count, BLOCK, head_count, diagonals * BLOCK),
        allowed,
        value_data.reshape(block_count, head_count, diagonals * BLOCK, head_width),
        "brjk,bjkd->brjd",
    )
    return (
        maximum.reshape(block_count * BLOCK, head_count),
        totals.reshape(block_count * BLOCK, head_count),
        summed.reshape(block_count * BLOCK, head_count, head_width),
    )


def shards(queries, new_keys, new_values, cache_keys, cache_values, verticals, offsets, out_weight):
    own_rows, head_count, head_width = queries.shape
    kv_heads = cache_keys.shape[1]
    ctx_size = lax.axis_size("ctx")
    ctx_index = lax.axis_index("ctx")
    cache_rows = cache_keys.shape[0]
    blocks_dev = cache_rows // BLOCK
    cache_blocks = blocks_dev * ctx_size
    own_blocks = own_rows // BLOCK
    scaling = 1.0 / math.sqrt(head_width)
    group_size = head_count // kv_heads
    tail_rows = SPAN * BLOCK
    piece_rows = min(cache_rows, tail_rows)
    holders = tail_rows // piece_rows
    stretch_keys, stretch_values = (
        lax.all_gather(new_keys, "ctx", axis=0, tiled=True),
        lax.all_gather(new_values, "ctx", axis=0, tiled=True),
    )
    tail_key_list = []
    tail_value_list = []
    for holder in range(holders):
        root = ctx_size - holders + holder
        tail_keys, tail_values = (
            from_root(cache_keys, "ctx", root),
            from_root(cache_values, "ctx", root),
        )
        tail_key_list.append(tail_keys)
        tail_value_list.append(tail_values)
    recent_keys = jnp.concatenate(tail_key_list + [stretch_keys], axis=0)
    recent_values = jnp.concatenate(tail_value_list + [stretch_values], axis=0)
    own_ids = ctx_index * own_blocks + jnp.arange(own_blocks, dtype=jnp.int32)
    slash_terms = slash_part(queries, own_ids, recent_keys, recent_values, offsets, scaling)
    global_block, local_block = local_slots(verticals, ctx_index * blocks_dev, blocks_dev)
    kv_index = (jnp.arange(head_count, dtype=jnp.int32) // group_size)[:, None]
    cache_key_blocks = cache_keys.reshape(blocks_dev, BLOCK, kv_heads, head_width)
    cache_value_blocks = cache_values.reshape(blocks_dev, BLOCK, kv_heads, head_width)
    slot_keys = cache_key_blocks[local_block, :, kv_index, :]
    slot_values = cache_value_blocks[local_block, :, kv_index, :]
    gathered_keys, gathered_values, gathered_blocks = (
        lax.all_gather(slot_keys, "ctx", axis=1, tiled=True),
        lax.all_gather(slot_values, "ctx", axis=1, tiled=True),
        lax.all_gather(global_block, "ctx", axis=1, tiled=True),
    )
    vertical = vertical_part(
        queries,
        own_ids,
        gathered_keys,
        gathered_values,
        gathered_blocks,
        offsets,
        cache_blocks,
        scaling,
    )
    maximum, totals, summed = merge_pair(vertical, slash_terms)
    attended = (
        (summed / totals[..., None]).astype(jnp.bfloat16).reshape(own_rows, head_count * head_width)
    )
    return lax.psum_scatter(
        jnp.dot(attended, out_weight, preferred_element_type=jnp.float32).astype(jnp.bfloat16),
        "kvh",
        scatter_dimension=0,
        tiled=True,
    )


def solution(mesh):
    return jax.shard_map(
        shards,
        mesh=mesh,
        in_specs=(
            P("ctx", "kvh", None),
            P("ctx", "kvh", None),
            P("ctx", "kvh", None),
            P("ctx", "kvh", None),
            P("ctx", "kvh", None),
            P("kvh", None),
            P("kvh", None),
            P("kvh", None),
        ),
        out_specs=P(("ctx", "kvh"), None),
        check_vma=False,
    )
```

profile of v0, /device:TPU:21, one launch (start us, length us, event | category | flops | bytes accessed | tf_op | source)
XLA Modules:
  0.0 843.9 jit_solution(3689525786264248457)
XLA Ops:
  7.5 0.8 convert_reduce_fusion
  8.5 5.4 copy.147
  13.9 3.5 gather_fusion.1
  17.4 10.0 %broadcast_select_fusion.2 = (bf16[8192,2,128]{2,0,1:T(8,128)(2,1)}, bf16[8192,2,128]{2,0,1:T(8,128)(2,1)}, bf16[8192,2,128]{2,0,1:T(8,128)(2,1)}, bf16[8192,2,128]{2,0,1:T(8,128)(2,1)}) fusion(pred[]{:T(512)S(6)} %eq.40, bf16[8192,2,128]{2,1,0:T(2,128)(2,1)} %param.12, pred[]{:T(512)S(6)} %eq.41, bf16[8192,2,128]{2,1,0:T(2,128)(2,1)} %param.11), kind=kLoop, calls=%fused_computation.23 | loop fusion | flops 8388608 | bytes 25165826 | tf_op jit(solution)/shard_map/jit(_where)/select_n | solution.py:17
  27.6 5.5 copy.144
  33.1 3.5 gather_fusion
  36.8 27.3 %all_gather.18 = bf16[1024,2,128]{2,0,1:T(8,128)(2,1)} all-gather(bf16[128,2,128]{2,0,1:T(8,128)(2,1)S(1)} %copy.156), channel_id=1, replica_groups=mesh['ctx'=8,'kvh'=4] {'ctx'}, dimensions={0}, use_global_device_ids=true | all-gather | bytes 589824 | tf_op jit(solution)/shard_map/all_gather | solution.py:126
  64.4 12.6 %all-gather = s32[8,2,8]{2,1,0:T(2,128)S(1)} all-gather(s32[1,2,8]{2,1,0:T(2,128)S(1)} %select_bitcast_fusion), channel_id=1, replica_groups=mesh['ctx'=8,'kvh'=4] {'ctx'}, dimensions={0}, use_global_device_ids=true | all-gather | bytes 576 | tf_op jit(solution)/shard_map/all_gather | solution.py:152
  77.5 1.1 broadcast_in_dim.37
  78.6 3.2 reshape.198
  81.8 2.5 copy.150
  84.4 29.0 %all_gather.19 = bf16[1024,2,128]{2,0,1:T(8,128)(2,1)S(1)} all-gather(bf16[128,2,128]{2,0,1:T(8,128)(2,1)S(1)} %copy.162), channel_id=1, replica_groups=mesh['ctx'=8,'kvh'=4] {'ctx'}, dimensions={0}, use_global_device_ids=true | all-gather | bytes 589824 | tf_op jit(solution)/shard_map/all_gather | solution.py:127
  113.5 1.4 or.39
  115.0 5.2 broadcast_or_fusion
  120.5 3.5 broadcast_or_fusion.1
  124.1 2.6 fusion.6
  126.6 2.0 copy-done.2
  128.6 1.3 fusion.7
  129.9 463.7 %all-reduce.3.cloned.1.call-done = (bf16[8192,2,128]{2,0,1:T(8,128)(2,1)}, bf16[8192,2,128]{2,0,1:T(8,128)(2,1)}, bf16[8192,2,128]{2,0,1:T(8,128)(2,1)}, bf16[8192,2,128]{2,0,1:T(8,128)(2,1)}) async-done(((bf16[8192,2,128]{2,0,1:T(8,128)(2,1)}, bf16[8192,2,128]{2,0,1:T(8,128)(2,1)}, bf16[8192,2,128]{2,0,1:T(8,128)(2,1)}, bf16[8192,2,128]{2,0,1:T(8,128)(2,1)}), (bf16[8192,2,128]{2,0,1:T(8,128)(2,1)}, ...) | async-done | bytes 16777232 | tf_op jit(solution)/shard_map/psum | solution.py:18
  593.6 13.5 %pad_maximum_fusion = bf16[17408,2,128]{2,0,1:T(8,128)(2,1)} fusion(bf16[1024,2,128]{2,0,1:T(8,128)(2,1)S(1)} %copy-done.3, bf16[8192,2,128]{2,0,1:T(8,128)(2,1)} %get-tuple-element.9, bf16[8192,2,128]{2,0,1:T(8,128)(2,1)} %get-tuple-element.10), kind=kLoop, calls=%fused_computation.15 | loop fusion | flops 26738688 | bytes 17825792 | tf_op jit(solution)/shard_map/concatenate | solution.py:139
  607.1 10.3 %copy.157 = bf16[272,64,2,128]{3,1,2,0:T(8,128)(2,1)} copy(bf16[272,64,2,128]{3,1,0,2:T(8,128)(2,1)} %bitcast.99) | data formatting | bytes 17825792 | tf_op jit(solution)/shard_map/reshape | solution.py:82
  617.3 25.3 %gather_fusion.2 = bf16[1536,64,128]{2,1,0:T(8,128)(2,1)} fusion(bf16[272,64,2,128]{3,1,2,0:T(8,128)(2,1)} %copy.157, s32[1536]{0:T(1024)S(1)} %reshape.222), kind=kCustom, calls=%fused_computation.2 | custom fusion | bytes 50343936 | tf_op jit(solution)/shard_map/gather | solution.py:86
  642.6 30.6 %fusion = (f32[2,64,8]{1,2,0:T(8,128)S(1)}, f32[2,8,96,64,64]{4,3,2,1,0:T(8,128)}) fusion(pred[64,8,96,64]{0,3,2,1:T(8,128)(4,1)} %broadcast_or_fusion, bf16[2,8,96,64,128]{4,3,2,1,0:T(8,128)(2,1)} %bitcast.101, bf16[2,64,8,128,1]{3,2,1,0,4:T(8,128)(2,1)S(1)} %bitcast.96), kind=kOutput, calls=%fused_computation.6 | convolution fusion | flops 1629486080 | bytes 53743616 | tf_op jit(solution)/shard_map/brjd,bjskd->brjsk/dot_general | solution.py:90
  673.2 22.6 %select_reduce_fusion = f32[2,64,8]{1,2,0:T(8,128)S(1)} fusion(f32[2,8,96,64,64]{4,3,2,1,0:T(8,128)} %get-tuple-element.23, f32[2,64,8]{1,2,0:T(8,128)S(1)} %get-tuple-element.22, pred[64,8,96,64]{0,3,2,1:T(8,128)(4,1)} %broadcast_or_fusion), kind=kLoop, calls=%fused_computation.5 | loop fusion | flops 25164800 | bytes 28319744 | tf_op jit(solution)/shard_map/reduce_sum | solution.py:25
  695.8 13.5 %pad_maximum_fusion.1 = bf16[17408,2,128]{2,0,1:T(8,128)(2,1)} fusion(bf16[1024,2,128]{2,0,1:T(8,128)(2,1)S(1)} %all_gather.19, bf16[8192,2,128]{2,0,1:T(8,128)(2,1)} %get-tuple-element.7, bf16[8192,2,128]{2,0,1:T(8,128)(2,1)} %get-tuple-element.8), kind=kLoop, calls=%fused_computation.16 | loop fusion | flops 26738688 | bytes 17825792 | tf_op jit(solution)/shard_map/concatenate | solution.py:140
  709.4 36.4 %copy.164 = f32[2,64,8,6144]{3,1,2,0:T(8,128)} copy(f32[2,64,8,6144]{1,3,2,0:T(8,128)} %bitcast.97) | data formatting | bytes 50331648 | tf_op jit(solution)/shard_map/reshape | solution.py:99
  745.9 10.2 %copy.163 = bf16[272,64,2,128]{3,1,2,0:T(8,128)(2,1)} copy(bf16[272,64,2,128]{3,1,0,2:T(8,128)(2,1)} %bitcast.98) | data formatting | bytes 17825792 | tf_op jit(solution)/shard_map/reshape | solution.py:83
  756.0 25.4 %gather_fusion.3 = bf16[1536,64,128]{2,1,0:T(8,128)(2,1)} fusion(bf16[272,64,2,128]{3,1,2,0:T(8,128)(2,1)} %copy.163, s32[1536]{0:T(1024)S(1)} %reshape.222), kind=kCustom, calls=%fused_computation.3 | custom fusion | bytes 50343936 | tf_op jit(solution)/shard_map/gather | solution.py:87
  781.4 19.3 %fusion.18 = f32[2,64,8,128]{3,1,2,0:T(8,128)S(1)} fusion(bf16[2,8,6144,128]{3,2,1,0:T(8,128)(2,1)} %bitcast.100, f32[2,64,8,6144]{3,1,2,0:T(8,128)} %copy.164, f32[2,64,8]{1,2,0:T(8,128)S(1)} %get-tuple-element.22, pred[64,8,6144]{2,0,1:T(8,128)(4,1)} %broadcast_or_fusion.1), kind=kOutput, calls=%fused_computation.34 | convolution fusion | flops 1635778560 | bytes 54005760 | tf_op jit(solution)/shard_map/brjk,bjkd->brjd/dot_general | solution.py:26
  801.3 4.8 fusion.28
  806.2 5.7 convolution_convert_fusion
  811.9 25.0 %reduce-scatter.2.cloned.1.call-done = bf16[32,4096]{1,0:T(8,128)(2,1)} async-done(((bf16[128,4096]{1,0:T(8,128)(2,1)}), bf16[32,4096]{1,0:T(8,128)(2,1)}) %reduce-scatter.2.cloned.1.call-update) | async-done | bytes 262160 | tf_op jit(solution)/shard_map/reduce_scatter | solution.py:168
  (56 shorter events, 3.5 us)
Async XLA Ops:
  6.5 117.5 %copy-start = (bf16[128,8,128]{2,1,0:T(8,128)(2,1)S(1)}, bf16[128,8,128]{2,1,0:T(8,128)(2,1)}, u32[]{:S(2)}) copy-start(bf16[128,8,128]{2,1,0:T(8,128)(2,1)} %param.8) | copy-start | bytes 786436
  6.5 117.5 %all-gather.6.cloned.1.call-start = ((), (), s32[]{:S(2)}) async-start(), calls=%async_computation.2 | async-start | bytes 2359296 | tf_op jit(solution)/shard_map/all_gather | solution.py:150
  17.4 576.2 %all-reduce.3.cloned.1.call-start = ((), (), s32[]{:S(2)}) async-start(), calls=%async_computation.4 | async-start | bytes 33554432 | tf_op jit(solution)/shard_map/psum | solution.py:18
  27.5 9.3 %copy-start.4 = (bf16[128,2,128]{2,1,0:T(2,128)(2,1)S(1)}, bf16[128,2,128]{2,1,0:T(2,128)(2,1)}, u32[]{:S(2)}) copy-start(bf16[128,2,128]{2,1,0:T(2,128)(2,1)} %param.9) | copy-start | bytes 196612
  27.5 36.6 %copy-start.6 = (s32[8,96]{1,0:T(8,128)S(1)}, s32[8,96]{1,0:T(8,128)}, u32[]{:S(2)}) copy-start(s32[8,96]{1,0:T(8,128)} %param.14) | copy-start | bytes 9220
  27.5 773.8 %all-gather.4.cloned.1.call-start = ((), (), s32[]{:S(2)}) async-start(), calls=%async_computation.1 | async-start | bytes 2359296 | tf_op jit(solution)/shard_map/all_gather | solution.py:151
  33.1 51.3 %copy-start.5 = (bf16[128,2,128]{2,1,0:T(2,128)(2,1)S(1)}, bf16[128,2,128]{2,1,0:T(2,128)(2,1)}, u32[]{:S(2)}) copy-start(bf16[128,2,128]{2,1,0:T(2,128)(2,1)} %param.10) | copy-start | bytes 196612
  36.6 800.3 %reduce-scatter.2.cloned.1.call-start = ((), (), s32[]{:S(2)}) async-start(), calls=%async_computation.3 | async-start | bytes 1310720 | tf_op jit(solution)/shard_map/reduce_scatter | solution.py:168
  124.1 469.5 %copy-start.3 = (bf16[1024,2,128]{2,0,1:T(8,128)(2,1)S(1)}, bf16[1024,2,128]{2,0,1:T(8,128)(2,1)}, u32[]{:S(2)}) copy-start(bf16[1024,2,128]{2,0,1:T(8,128)(2,1)} %all_gather.18) | copy-start | bytes 1572868
  126.6 2.0 copy-start.2
  806.2 30.8 %copy-start.1 = (bf16[128,8,128]{2,1,0:T(8,128)(2,1)S(1)}, bf16[128,8,128]{2,1,0:T(8,128)(2,1)}, u32[]{:S(2)}) copy-start(bf16[128,8,128]{2,1,0:T(8,128)(2,1)} %param.8) | copy-start | bytes 786436
Sparse Core Ops, SparseCore 0:
  17.5 54.6 all-gather.5
  77.0 516.5 all-reduce.2
  595.8 47.2 all-gather.3
  812.0 24.8 reduce-scatter.1
where the time goes:
time: 853 us; the launch traced here: 844 us
  waiting for transfers between devices  489 us (57%)
  local copies, waits for them, and re-layouts  137 us (16%)
  other arithmetic  72 us (8%)
  blocking collectives  68.8 us (8%)
  matrix products  63 us (7%)
  between operations  13.8 us (2%)
    psum x1, waiting for transfers between devices, from_root(): return lax.psum(block, axis)  464 us
    reshape x1, local copies, waits for them, and re-layouts, slash_part(): scores.reshape(block_count, BLOCK, head_count, diagonals * BLOCK)  36.4 us
    dot_general x1, matrix products, slash_part(): jnp.einsum('brjd,bjskd->brjsk', grouped, key_data, preferred_element_type...  30.6 us
    all_gather x1, blocking collectives, shards(): lax.all_gather(new_values, 'ctx', axis=0, tiled=True)  29 us
    all_gather x1, blocking collectives, shards(): lax.all_gather(new_keys, 'ctx', axis=0, tiled=True)  27.3 us
    gather x1, local copies, waits for them, and re-layouts, slash_part(): value_data = value_blocks[where_block, :, kv_index, :]  25.4 us
    gather x1, local copies, waits for them, and re-layouts, slash_part(): key_data = key_blocks[where_block, :, kv_index, :]  25.3 us
    reduce_scatter x1, waiting for transfers between devices, shards(): lax.psum_scatter(jnp.dot(attended, out_weight, preferred_element_type=jnp...  25 us
  transfers between devices with their start and end apart: 4, of which 2 were waited for; matrix products, arithmetic and copies ran while one was open for 30% of the time, Pallas kernels for 0%

commit v1 on v0

v1 whole, which is shorter than its diff:
```python
import functools
import math

import jax
import jax.numpy as jnp
from jax import lax
from jax.experimental import pallas as pl
from jax.experimental.pallas import tpu as pltpu
from jax.sharding import PartitionSpec as P

BLOCK = 64
SPAN = 256
VCAP = 2
GROUP = 8
LOWEST = -1e30
MESH = pl.DeviceIdType.MESH
VMEM_LIMIT = 56 * 1024 * 1024


def lane_fold(x, op):
    parts = [x[:, i * 128 : (i + 1) * 128] for i in range(x.shape[1] // 128)]
    return functools.reduce(op, parts)


def to_row(column):
    return jnp.transpose(jnp.broadcast_to(column, (column.shape[0], 128)))[0:1, :]


def slash_kernel(
    factor, heads, base_ref, off_ref, lo_ref, hi_ref, q_ref, k_ref, v_ref, o_ref, lse_ref, s_ref
):
    kv = pl.program_id(0)
    key_blocks = k_ref.shape[1] // BLOCK
    diagonals = off_ref.shape[1]
    owners = q_ref.shape[0]
    width = GROUP * BLOCK

    def one_pair(it, carry):
        hh = it // owners
        c = it - hh * owners
        h = kv * heads + hh
        spans = [(lo_ref[h, 2 * c + i], hi_ref[h, 2 * c + i]) for i in range(2)]
        counts = [hi - lo for lo, hi in spans]
        groups = lax.div(jnp.maximum(counts[0], counts[1]) + (GROUP - 1), GROUP)

        def gathered(ref, i, t):
            lo, hi = spans[i]
            rows = []
            for g in range(GROUP):
                slot = jnp.clip(jnp.minimum(lo + t * GROUP + g, hi - 1), 0, diagonals - 1)
                j = jnp.clip(base_ref[0] + 2 * c + i - off_ref[h, slot], 0, key_blocks - 1)
                rows.append(ref[0, pl.ds(pl.multiple_of(j * BLOCK, BLOCK), BLOCK), :])
            return jnp.concatenate(rows, axis=0)

        q = [q_ref[c, hh, i * BLOCK : (i + 1) * BLOCK, :] for i in range(2)]

        def first(t, best):
            new = []
            for i in range(2):
                s = lax.dot_general(
                    q[i],
                    gathered(k_ref, i, t),
                    (((1,), (1,)), ((), ())),
                    preferred_element_type=jnp.float32,
                )
                s_ref[i, t] = s
                new.append(jnp.maximum(best[i], lane_fold(s, jnp.maximum)))
            return tuple(new)

        low = jnp.full((BLOCK, 128), LOWEST, jnp.float32)
        best = lax.fori_loop(0, groups, first, (low, low))

        @pl.when(groups > 0)
        def _():
            key = lax.broadcasted_iota(jnp.int32, (BLOCK, width), 1)
            for i in range(2):
                valid = (counts[i] - (groups - 1) * GROUP) * BLOCK
                s_ref[i, groups - 1] = jnp.where(key < valid, s_ref[i, groups - 1], LOWEST)

        top = [jnp.max(b, axis=1, keepdims=True) for b in best]

        def second(t, state):
            new = []
            for i in range(2):
                total, acc = state[i]
                p = jnp.exp2((s_ref[i, t] - top[i]) * factor)
                total = total + lane_fold(p, jnp.add)
                acc = acc + jnp.dot(
                    p.astype(jnp.bfloat16), gathered(v_ref, i, t), preferred_element_type=jnp.float32
                )
                new.append((total, acc))
            return tuple(new)

        zero = jnp.zeros((BLOCK, 128), jnp.float32)
        state = lax.fori_loop(0, groups, second, ((zero, zero), (zero, zero)))
        lse = []
        for i in range(2):
            total = jnp.sum(state[i][0], axis=1, keepdims=True)
            some = total > 0.0
            safe = jnp.where(some, total, 1.0)
            o_ref[c, hh, i * BLOCK : (i + 1) * BLOCK, :] = (state[i][1] / safe).astype(o_ref.dtype)
            lse.append(jnp.where(some, top[i] * factor + jnp.log2(safe), LOWEST))
        lse_ref[c, 0, pl.ds(hh, 1), :] = to_row(jnp.concatenate(lse, axis=0))
        return carry

    lax.fori_loop(0, heads * owners, one_pair, 0)


def slash_attention(base, sorted_offsets, lo, hi, queries, keys, values, factor):
    owners, head_count, rows, hd = queries.shape
    kv_heads, key_rows, _ = keys.shape
    heads = head_count // kv_heads
    most = -(-sorted_offsets.shape[1] // GROUP)
    elements = head_count * rows * owners * 48 * BLOCK
    return pl.pallas_call(
        functools.partial(slash_kernel, factor, heads),
        grid_spec=pltpu.PrefetchScalarGridSpec(
            num_scalar_prefetch=4,
            grid=(kv_heads,),
            in_specs=[
                pl.BlockSpec((owners, heads, rows, hd), lambda g, *_: (0, g, 0, 0)),
                pl.BlockSpec((1, key_rows, hd), lambda g, *_: (g, 0, 0)),
                pl.BlockSpec((1, key_rows, hd), lambda g, *_: (g, 0, 0)),
            ],
            out_specs=[
                pl.BlockSpec((owners, heads, rows, hd), lambda g, *_: (0, g, 0, 0)),
                pl.BlockSpec((owners, 1, heads, rows), lambda g, *_: (0, g, 0, 0)),
            ],
            scratch_shapes=[pltpu.VMEM((2, most, BLOCK, GROUP * BLOCK), jnp.float32)],
        ),
        out_shape=[
            jax.ShapeDtypeStruct(queries.shape, jnp.bfloat16),
            jax.ShapeDtypeStruct((owners, kv_heads, heads, rows), jnp.float32),
        ],
        compiler_params=pltpu.CompilerParams(vmem_limit_bytes=VMEM_LIMIT),
        cost_estimate=pl.CostEstimate(
            flops=4 * elements * hd, bytes_accessed=12 * 2**20, transcendentals=elements
        ),
    )(base, sorted_offsets, lo, hi, queries, keys, values)


def local_kernel(factor, me_ref, q_ref, kv_ref, vv_ref, kn_ref, vn_ref, bias_ref, o_ref, lse_ref):
    rows, hd = q_ref.shape[1:]
    blocks = rows // BLOCK

    def flat(ref):
        return ref[...].reshape(-1, hd)

    def scores(keys, kind):
        s = lax.dot_general(
            q_ref[0], keys, (((1,), (1,)), ((), ())), preferred_element_type=jnp.float32
        )
        bias = bias_ref[0, kind]
        parts = [s[i * BLOCK : (i + 1) * BLOCK] + bias[i : i + 1] for i in range(blocks)]
        return jnp.concatenate(parts, axis=0)

    s_vert = scores(flat(kv_ref), 0)
    s_new = scores(flat(kn_ref), 1)
    key = lax.broadcasted_iota(jnp.int32, s_new.shape, 1)
    row = lax.broadcasted_iota(jnp.int32, s_new.shape, 0) + me_ref[0] * rows
    s_new = jnp.where(key <= row, s_new, LOWEST)
    top = jnp.maximum(
        jnp.max(lane_fold(s_vert, jnp.maximum), axis=1, keepdims=True),
        jnp.max(lane_fold(s_new, jnp.maximum), axis=1, keepdims=True),
    )
    p_vert = jnp.exp2((s_vert - top) * factor)
    p_new = jnp.exp2((s_new - top) * factor)
    total = jnp.sum(lane_fold(p_vert, jnp.add) + lane_fold(p_new, jnp.add), axis=1, keepdims=True)
    acc = jnp.dot(
        p_vert.astype(jnp.bfloat16), flat(vv_ref), preferred_element_type=jnp.float32
    ) + jnp.dot(p_new.astype(jnp.bfloat16), flat(vn_ref), preferred_element_type=jnp.float32)
    o_ref[0] = acc / total
    lse_ref[0] = to_row(top * factor + jnp.log2(total))


def local_attention(me, queries, gathered, bias, kv_heads, factor):
    head_count, rows, hd = queries.shape
    owners = gathered.shape[0]
    blocks = rows // BLOCK
    group = head_count // kv_heads
    piece = (owners, 2, BLOCK, hd)
    return pl.pallas_call(
        functools.partial(local_kernel, factor),
        grid_spec=pltpu.PrefetchScalarGridSpec(
            num_scalar_prefetch=1,
            grid=(head_count,),
            in_specs=[
                pl.BlockSpec((1, rows, hd), lambda h, *_: (h, 0, 0)),
                pl.BlockSpec(piece, lambda h, *_: (0, h, 0, 0)),
                pl.BlockSpec(piece, lambda h, *_: (0, head_count + h, 0, 0)),
                pl.BlockSpec(piece, lambda h, *_: (0, 2 * head_count + h // group, 0, 0)),
                pl.BlockSpec(piece, lambda h, *_: (0, 2 * head_count + kv_heads + h // group, 0, 0)),
                pl.BlockSpec((1, 2, blocks, bias.shape[-1]), lambda h, *_: (h, 0, 0, 0)),
            ],
            out_specs=[
                pl.BlockSpec((1, rows, hd), lambda h, *_: (h, 0, 0)),
                pl.BlockSpec((1, 1, rows), lambda h, *_: (h, 0, 0)),
            ],
        ),
        out_shape=[
            jax.ShapeDtypeStruct(queries.shape, jnp.float32),
            jax.ShapeDtypeStruct((head_count, 1, rows), jnp.float32),
        ],
        compiler_params=pltpu.CompilerParams(vmem_limit_bytes=VMEM_LIMIT),
        cost_estimate=pl.CostEstimate(
            flops=4 * head_count * rows * hd * 2 * bias.shape[-1],
            bytes_accessed=6 * 2**20,
            transcendentals=head_count * rows * 2 * bias.shape[-1],
        ),
    )(me, queries, gathered, gathered, gathered, gathered, bias)


def return_kernel(holders, o_ref, l_ref, part_ref, plse_ref, o_send, l_send, o_recv, l_recv, o_own, l_own):
    size = lax.axis_size("ctx")
    me = lax.axis_index("ctx")
    kvh = lax.axis_index("kvh")
    first = size - holders
    barrier = pltpu.get_barrier_semaphore()
    for r in range(holders):

        @pl.when(me != first + r)
        def _():
            pl.semaphore_signal(barrier, inc=1, device_id=(first + r, kvh), device_id_type=MESH)

    def copies(r, step):
        to = lax.rem(me + step, size)
        pairs = ((o_ref, part_ref, o_send, o_recv), (l_ref, plse_ref, l_send, l_recv))
        return [
            pltpu.make_async_remote_copy(
                src_ref=src.at[to],
                dst_ref=dst.at[r],
                send_sem=send.at[step - 1],
                recv_sem=recv.at[r],
                device_id=(to, kvh),
                device_id_type=MESH,
            )
            for src, dst, send, recv in pairs
        ]

    for r in range(holders):

        @pl.when(me == first + r)
        def _():
            pl.semaphore_wait(barrier, size - 1)
            for step in range(1, size):
                for copy in copies(r, step):
                    copy.start()
            own = [
                pltpu.make_async_copy(o_ref.at[me], part_ref.at[r], o_own),
                pltpu.make_async_copy(l_ref.at[me], plse_ref.at[r], l_own),
            ]
            for copy in own:
                copy.start()
            for copy in own:
                copy.wait()
            for step in range(1, size):
                for copy in copies(r, step):
                    copy.wait_send()

    for r in range(holders):

        @pl.when(me != first + r)
        def _():
            for copy in copies(r, 1):
                copy.wait_recv()


def return_parts(o, lse, holders):
    size = o.shape[0]
    return pl.pallas_call(
        functools.partial(return_kernel, holders),
        out_shape=[
            jax.ShapeDtypeStruct((holders,) + o.shape[1:], o.dtype),
            jax.ShapeDtypeStruct((holders,) + lse.shape[1:], lse.dtype),
        ],
        in_specs=[pl.BlockSpec(memory_space=pl.ANY)] * 2,
        out_specs=[pl.BlockSpec(memory_space=pl.ANY)] * 2,
        scratch_shapes=[
            pltpu.SemaphoreType.DMA((size - 1,)),
            pltpu.SemaphoreType.DMA((size - 1,)),
            pltpu.SemaphoreType.DMA((holders,)),
            pltpu.SemaphoreType.DMA((holders,)),
            pltpu.SemaphoreType.DMA,
            pltpu.SemaphoreType.DMA,
        ],
        compiler_params=pltpu.CompilerParams(collective_id=0, has_side_effects=True),
    )(o, lse)


def slots_of(verticals, lower_block, blocks_dev):
    inside = (verticals >= lower_block) & (verticals < lower_block + blocks_dev)
    counts = inside.astype(jnp.int32)
    slot_rank = jnp.cumsum(counts, axis=1) - counts
    slot_ids = jnp.arange(VCAP, dtype=jnp.int32)
    onehot = inside[:, None, :] & (slot_rank[:, None, :] == slot_ids[None, :, None])
    filled = jnp.any(onehot, axis=2)
    block = jnp.sum(jnp.where(onehot, verticals[:, None, :], 0), axis=2)
    return jnp.where(filled, block, -1)


def shards(queries, new_keys, new_values, cache_keys, cache_values, verticals, offsets, out_weight):
    own_rows, head_count, hd = queries.shape
    kv_heads = cache_keys.shape[1]
    size = lax.axis_size("ctx")
    me = lax.axis_index("ctx")
    cache_rows = cache_keys.shape[0]
    blocks_dev = cache_rows // BLOCK
    cache_blocks = blocks_dev * size
    own_blocks = own_rows // BLOCK
    holders = SPAN // blocks_dev
    group = head_count // kv_heads
    factor = math.log2(math.e) / math.sqrt(hd)

    q_own = jnp.transpose(queries, (1, 0, 2))
    q_all = lax.all_gather(q_own, "ctx", axis=0, tiled=False)

    keys = jnp.transpose(cache_keys, (1, 0, 2))
    values = jnp.transpose(cache_values, (1, 0, 2))
    mine = slots_of(verticals, me * blocks_dev, blocks_dev)
    local_block = jnp.where(mine >= 0, mine - me * blocks_dev, 0)
    kv_of = (jnp.arange(head_count, dtype=jnp.int32) // group)[:, None]
    flat_block = (kv_of * blocks_dev + local_block).reshape(-1)
    slot_keys = keys.reshape(-1, BLOCK, hd)[flat_block]
    slot_values = values.reshape(-1, BLOCK, hd)[flat_block]
    fresh_keys = jnp.transpose(new_keys, (1, 0, 2)).reshape(-1, BLOCK, hd)
    fresh_values = jnp.transpose(new_values, (1, 0, 2)).reshape(-1, BLOCK, hd)
    packed = jnp.concatenate([slot_keys, slot_values, fresh_keys, fresh_values], axis=0)
    gathered = lax.all_gather(packed, "ctx", axis=0, tiled=False)

    rank = jnp.sum((offsets[:, :, None] > offsets[:, None, :]).astype(jnp.int32), axis=2)
    places = jnp.arange(offsets.shape[1], dtype=jnp.int32)
    sorted_offsets = jnp.sum(
        jnp.where(rank[:, :, None] == places[None, None, :], offsets[:, :, None], 0), axis=1
    )
    holder = me - (size - holders)
    base = SPAN - holder * blocks_dev
    block_ids = jnp.arange(size * own_blocks, dtype=jnp.int32)
    highest = (base + block_ids)[None, :, None]
    hi = jnp.sum((offsets[:, None, :] <= highest).astype(jnp.int32), axis=2)
    lo = jnp.sum((offsets[:, None, :] <= highest - blocks_dev).astype(jnp.int32), axis=2)
    is_holder = holder >= 0
    lo = jnp.where(is_holder, lo, 0)
    hi = jnp.where(is_holder, hi, 0)
    slash_o, slash_lse = slash_attention(
        base.reshape(1), sorted_offsets, lo, hi, q_all, keys, values, factor
    )
    part_o, part_lse = return_parts(slash_o, slash_lse, holders)

    own_ids = me * own_blocks + jnp.arange(own_blocks, dtype=jnp.int32)
    slots = jnp.stack([slots_of(verticals, c * blocks_dev, blocks_dev) for c in range(size)], axis=1)
    slots = slots.reshape(head_count, size * VCAP)
    slash_blocks = cache_blocks + own_ids[None, :, None] - offsets[:, None, :]
    repeated = jnp.any(slots[:, None, :, None] == slash_blocks[:, :, None, :], axis=-1)
    vert_ok = (slots[:, None, :] >= 0) & jnp.logical_not(repeated)
    new_ids = cache_blocks + jnp.arange(size * own_blocks, dtype=jnp.int32)
    new_ok = jnp.any(new_ids[None, None, :, None] == slash_blocks[:, :, None, :], axis=-1)
    bias = jnp.where(jnp.stack([vert_ok, new_ok], axis=1), 0.0, LOWEST).astype(jnp.float32)
    bias = jnp.repeat(bias, BLOCK, axis=-1)
    own_o, own_lse = local_attention(me.reshape(1), q_own, gathered, bias, kv_heads, factor)

    own_lse = own_lse.reshape(head_count, own_rows)
    part_lse = part_lse.reshape(holders, head_count, own_rows)
    top = jnp.maximum(own_lse, jnp.max(part_lse, axis=0))
    own_share = jnp.exp2(own_lse - top)
    part_share = jnp.exp2(part_lse - top[None])
    whole = own_share + jnp.sum(part_share, axis=0)
    mixed = own_o * (own_share / whole)[..., None] + jnp.sum(
        part_o.astype(jnp.float32) * (part_share / whole[None])[..., None], axis=0
    )
    attended = jnp.transpose(mixed.astype(jnp.bfloat16), (1, 0, 2)).reshape(own_rows, head_count * hd)
    return lax.psum_scatter(
        jnp.dot(attended, out_weight, preferred_element_type=jnp.float32).astype(jnp.bfloat16),
        "kvh",
        scatter_dimension=0,
        tiled=True,
    )


def solution(mesh):
    return jax.shard_map(
        shards,
        mesh=mesh,
        in_specs=(
            P("ctx", "kvh", None),
            P("ctx", "kvh", None),
            P("ctx", "kvh", None),
            P("ctx", "kvh", None),
            P("ctx", "kvh", None),
            P("kvh", None),
            P("kvh", None),
            P("kvh", None),
        ),
        out_specs=P(("ctx", "kvh"), None),
        check_vma=False,
    )
```

time: 853 us -> 381 us (0.45); the launches traced: 844 us -> 382 us
  waiting for transfers between devices: 489 us -> 48 us
  Pallas kernels: 0 us -> 284 us
  local copies, waits for them, and re-layouts: 137 us -> 17.9 us
  blocking collectives: 68.8 us -> 0 us
  other arithmetic: 72 us -> 13.2 us
  matrix products: 63 us -> 5.66 us
    psum x1 -> x0, waiting for transfers between devices: 464 us -> none  [from_root(): return lax.psum(block, axis)]
    pallas_call x0 -> x3, Pallas kernels: none -> 284 us  [the longest x1 248 us: return_parts(): pl.pallas_call(functools.partial(return_kernel, holders), out_shape=[jax....]
    reshape x10 -> x1, local copies, waits for them, and re-layouts: 73.8 us -> 0.81 us  [shards(): bias = jnp.repeat(bias, BLOCK, axis=-1)]
    all_gather x3 -> x0, blocking collectives: 68.8 us -> none  [the longest x1 29 us: shards(): lax.all_gather(new_values, 'ctx', axis=0, tiled=True)]
    dot_general x4 -> x0, matrix products: 57.3 us -> none  [the longest x1 30.6 us: slash_part(): jnp.einsum('brjd,bjskd->brjsk', grouped, key_data, preferred_element_type...]
    gather x4 -> x2, local copies, waits for them, and re-layouts: 57.7 us -> 5.6 us  [the longest x1 2.81 us: shards(): slot_values = values.reshape(-1, BLOCK, hd)[flat_block]]
    concatenate x6 -> x1, other arithmetic: 27.1 us -> 0.94 us  [shards(): jnp.concatenate([slot_keys, slot_values, fresh_keys, fresh_values], axis=0)]
    all_gather x2, waiting for transfers between devices: 0.02 us -> 24.4 us  [the longest x1 24.4 us: shards(): q_all = lax.all_gather(q_own, 'ctx', axis=0, tiled=False)]
  transfers between devices with their start and end apart: 4 -> 3, of which waited for: 2 -> 2; matrix products, arithmetic and copies ran while one was open for 30% -> 7% of each run, Pallas kernels for 0% -> 72%
where the time goes in v1:
time: 381 us; the launch traced here: 382 us
  Pallas kernels  284 us (75%)
  waiting for transfers between devices  48 us (13%)
  local copies, waits for them, and re-layouts  17.9 us (5%)
  between operations  13.4 us (4%)
  other arithmetic  13.2 us (3%)
  matrix products  5.66 us (1%)
    pallas_call x1, Pallas kernels, return_parts(): pl.pallas_call(functools.partial(return_kernel, holders), out_shape=[jax....  248 us
    pallas_call x1, Pallas kernels, slash_attention(): pl.pallas_call(functools.partial(slash_kernel, factor, heads), grid_spec=...  26.5 us
    all_gather x1, waiting for transfers between devices, shards(): q_all = lax.all_gather(q_own, 'ctx', axis=0, tiled=False)  24.4 us
    reduce_scatter x1, waiting for transfers between devices, shards(): lax.psum_scatter(jnp.dot(attended, out_weight, preferred_element_type=jnp...  23.6 us
    unnamed x14, local copies, waits for them, and re-layouts  11 us
    pallas_call x1, Pallas kernels, local_attention(): pl.pallas_call(functools.partial(local_kernel, factor), grid_spec=pltpu.P...  9.27 us
  transfers between devices with their start and end apart: 3, of which 2 were waited for; matrix products, arithmetic and copies ran while one was open for 7% of the time, Pallas kernels for 72%

profile of v1, /device:TPU:21, one launch (start us, length us, event | category | flops | bytes accessed | tf_op | source)
XLA Modules:
  0.0 381.9 jit_solution(9674965261634137954)
XLA Ops:
  6.5 1.7 copy.48
  8.3 0.7 fusion.24
  9.0 0.2 reduce_window_sum.55
  9.2 0.2 reduce_window_sum.51
  9.4 0.2 reduce_window_sum.50
  9.9 0.2 reduce_window_sum.44
  10.0 0.2 reduce_window_sum.43
  10.8 1.1 select_reduce_fusion.1
  12.1 9.2 %fusion.33 = (bf16[8192,2,128]{2,0,1:T(8,128)(2,1)}, bf16[2,8192,128]{2,1,0:T(8,128)(2,1)}, bf16[2,8192,128]{2,1,0:T(8,128)(2,1)}, bf16[8192,2,128]{2,0,1:T(8,128)(2,1)}) fusion(bf16[8192,2,128]{2,1,0:T(2,128)(2,1)} %param.11, bf16[8192,2,128]{2,1,0:T(2,128)(2,1)} %param.12), kind=kLoop, calls=%fused_computation.113 | loop fusion | bytes 25165824 | tf_op args[3]
  21.3 2.8 gather_fusion
  24.1 2.8 gather_fusion.1
  27.0 0.9 pad_maximum_fusion
  28.9 0.7 compare_reduce_fusion.1
  29.8 0.8 reshape.339.bias_ref
  30.6 0.4 convert_reduce_fusion.1
  31.1 0.4 convert_reduce_fusion
  31.4 0.9 select_reduce_fusion.off_ref
  32.3 0.6 broadcast_select_fusion.hi_ref
  32.9 0.6 broadcast_select_fusion.1.lo_ref
  33.5 24.4 %all-gather.7.cloned.1.call-done = bf16[64,128,128]{2,1,0:T(8,128)(2,1)} async-done(((bf16[8,128,128]{2,1,0:T(8,128)(2,1)}), bf16[64,128,128]{2,1,0:T(8,128)(2,1)}) %all-gather.7.cloned.1.call-update) | async-done | bytes 2097168 | tf_op jit(solution)/shard_map/all_gather | solution.py:315
  57.8 26.5 %shard_map.83 = (bf16[8,8,128,128]{3,2,1,0:T(8,128)(2,1)}, f32[8,2,4,128]{3,2,1,0:T(4,128)}) custom-call(s32[1]{0:T(128)} %bitcast.24.base_ref, s32[8,96]{1,0:T(8,128)} %select_reduce_fusion.off_ref, s32[8,16]{1,0:T(8,128)} %broadcast_select_fusion.1.lo_ref, s32[8,16]{1,0:T(8,128)} %broadcast_select_fusion.hi_ref, bf16[8,8,128,128]{3,2,1,0:T(8,128)(2,1)} %bitcast.75, ...), custom_call_target="tpu_custom_call" | custom-call | flops 12884901888 | bytes 12582912 | tf_op jit(solution)/shard_map/pallas_call | solution.py:115
  84.4 247.8 %shard_map.84 = (bf16[2,8,128,128]{3,2,1,0:T(8,128)(2,1)}, f32[2,2,4,128]{3,2,1,0:T(4,128)}) custom-call(bf16[8,8,128,128]{3,2,1,0:T(8,128)(2,1)} %get-tuple-element.13.o_ref, f32[8,2,4,128]{3,2,1,0:T(4,128)} %get-tuple-element.14.l_ref), custom_call_target="tpu_custom_call" | custom-call | tf_op jit(solution)/shard_map/pallas_call | solution.py:270
  332.2 0.7 reduce_max.11
  332.9 9.3 %shard_map.82 = (f32[8,128,128]{2,1,0:T(8,128)}, f32[8,1,128]{2,1,0:T(1,128)}) custom-call(s32[1]{0:T(128)} %bitcast.me_ref, bf16[8,128,128]{2,1,0:T(8,128)(2,1)} %bitcast.62, bf16[8,40,64,128]{3,2,1,0:T(8,128)(2,1)} %bitcast.55, bf16[8,40,64,128]{3,2,1,0:T(8,128)(2,1)} %bitcast.56, bf16[8,40,64,128]{3,2,1,0:T(8,128)(2,1)} %bitcast.57, ...), custom_call_target="tpu_custom_call" | custom-call | flops 1073741824 | bytes 6291456 | tf_op jit(solution)/shard_map/pallas_call | solution.py:182
  342.2 0.7 max.18
  342.9 0.7 fusion.19
  343.6 0.7 fusion.20
  344.3 0.3 multiply_reduce_fusion
  344.6 1.2 fusion
  345.9 0.2 copy.42
  346.1 5.7 %convolution_convert_fusion = bf16[128,4096]{1,0:T(8,128)(2,1)} fusion(bf16[128,1024]{0,1:T(8,128)(2,1)S(1)} %bitcast.63, bf16[1024,4096]{1,0:T(8,128)(2,1)} %param.15), kind=kOutput, calls=%fused_computation.2 | convolution fusion | flops 1074266112 | bytes 9699328 | tf_op jit(solution)/shard_map/dot_general | solution.py:372
  351.8 23.6 %reduce-scatter.2.cloned.1.call-done = bf16[32,4096]{1,0:T(8,128)(2,1)} async-done(((bf16[128,4096]{1,0:T(8,128)(2,1)}), bf16[32,4096]{1,0:T(8,128)(2,1)}) %reduce-scatter.2.cloned.1.call-update) | async-done | bytes 262160 | tf_op jit(solution)/shard_map/reduce_scatter | solution.py:371
  (63 shorter events, 2.3 us)
Async XLA Ops:
  6.5 51.3 %all-gather.7.cloned.1.call-start = ((), (), s32[]{:S(2)}) async-start(), calls=%async_computation.3 | async-start | bytes 2359296 | tf_op jit(solution)/shard_map/all_gather | solution.py:315
  8.2 324.7 %all-gather.5.cloned.1.call-start = ((), (), s32[]{:S(2)}) async-start(), calls=%async_computation.2 | async-start | bytes 5898240 | tf_op jit(solution)/shard_map/all_gather | solution.py:328
  12.0 14.9 %copy-start.3 = (bf16[128,2,128]{2,1,0:T(2,128)(2,1)S(1)}, bf16[128,2,128]{2,1,0:T(2,128)(2,1)}, u32[]{:S(2)}) copy-start(bf16[128,2,128]{2,1,0:T(2,128)(2,1)} %param.10) | copy-start | bytes 196612
  12.1 14.9 %copy-start.4 = (bf16[128,2,128]{2,1,0:T(2,128)(2,1)S(1)}, bf16[128,2,128]{2,1,0:T(2,128)(2,1)}, u32[]{:S(2)}) copy-start(bf16[128,2,128]{2,1,0:T(2,128)(2,1)} %param.9) | copy-start | bytes 196612
  12.1 16.8 %copy-start.1 = (s32[8,96]{1,0:T(8,128)S(1)}, s32[8,96]{1,0:T(8,128)}, u32[]{:S(2)}) copy-start(s32[8,96]{1,0:T(8,128)} %param.14) | copy-start | bytes 9220
  28.0 347.4 %reduce-scatter.2.cloned.1.call-start = ((), (), s32[]{:S(2)}) async-start(), calls=%async_computation.1 | async-start | bytes 1310720 | tf_op jit(solution)/shard_map/reduce_scatter | solution.py:371
  332.9 10.0 %copy-start.2 = (f32[2,2,4,128]{3,2,1,0:T(4,128)S(1)}, f32[2,2,4,128]{3,2,1,0:T(4,128)}, u32[]{:S(2)}) copy-start(f32[2,2,4,128]{3,2,1,0:T(4,128)} %get-tuple-element.15) | copy-start | bytes 24580
  332.9 11.4 %copy-start = (bf16[2,8,128,128]{3,2,1,0:T(8,128)(2,1)S(1)}, bf16[2,8,128,128]{3,2,1,0:T(8,128)(2,1)}, u32[]{:S(2)}) copy-start(bf16[2,8,128,128]{3,2,1,0:T(8,128)(2,1)} %get-tuple-element.16) | copy-start | bytes 1572868
Sparse Core Ops, SparseCore 0:
  9.5 48.3 all-gather.6
  60.0 84.6 all-gather.4
  351.9 23.4 reduce-scatter.1

commit v2 on v1

--- a/solution.py
+++ b/solution.py
@@ -11,7 +11,8 @@
 BLOCK = 64
 SPAN = 256
 VCAP = 2
-GROUP = 8
+GROUP = 12
+BUNDLE = 4
 LOWEST = -1e30
 MESH = pl.DeviceIdType.MESH
 VMEM_LIMIT = 56 * 1024 * 1024
@@ -27,95 +28,99 @@
 
 
 def slash_kernel(
-    factor, heads, base_ref, off_ref, lo_ref, hi_ref, q_ref, k_ref, v_ref, o_ref, lse_ref, s_ref
+    factor, heads, length, list_ref, count_ref, q_ref, k_ref, v_ref, o_ref, lse_ref, s_ref
 ):
     kv = pl.program_id(0)
-    key_blocks = k_ref.shape[1] // BLOCK
-    diagonals = off_ref.shape[1]
     owners = q_ref.shape[0]
     width = GROUP * BLOCK
-
-    def one_pair(it, carry):
-        hh = it // owners
-        c = it - hh * owners
-        h = kv * heads + hh
-        spans = [(lo_ref[h, 2 * c + i], hi_ref[h, 2 * c + i]) for i in range(2)]
-        counts = [hi - lo for lo, hi in spans]
-        groups = lax.div(jnp.maximum(counts[0], counts[1]) + (GROUP - 1), GROUP)
-
-        def gathered(ref, i, t):
-            lo, hi = spans[i]
-            rows = []
-            for g in range(GROUP):
-                slot = jnp.clip(jnp.minimum(lo + t * GROUP + g, hi - 1), 0, diagonals - 1)
-                j = jnp.clip(base_ref[0] + 2 * c + i - off_ref[h, slot], 0, key_blocks - 1)
-                rows.append(ref[0, pl.ds(pl.multiple_of(j * BLOCK, BLOCK), BLOCK), :])
+    bundle = min(BUNDLE, heads)
+    chains = [(a, i) for a in range(bundle) for i in range(2)]
+
+    def one_bundle(it, carry):
+        first_head = (it // owners) * bundle
+        c = lax.rem(it, owners)
+        hh = [first_head + a for a, _ in chains]
+        block = [2 * c + i for _, i in chains]
+        pair = [(kv * heads + h) * (2 * owners) + b for h, b in zip(hh, block)]
+        counts = [count_ref[p] for p in pair]
+        most = functools.reduce(jnp.maximum, counts)
+        groups = lax.div(most + (GROUP - 1), GROUP)
+
+        def gathered(ref, n, t):
+            at = pair[n] * length + t * GROUP
+            rows = [
+                ref[0, pl.ds(pl.multiple_of(list_ref[at + g], BLOCK), BLOCK), :] for g in range(GROUP)
+            ]
             return jnp.concatenate(rows, axis=0)
-
-        q = [q_ref[c, hh, i * BLOCK : (i + 1) * BLOCK, :] for i in range(2)]
 
         def first(t, best):
             new = []
-            for i in range(2):
+            for n, (_, i) in enumerate(chains):
                 s = lax.dot_general(
-                    q[i],
-                    gathered(k_ref, i, t),
+                    q_ref[c, hh[n], i * BLOCK : (i + 1) * BLOCK, :],
+                    gathered(k_ref, n, t),
                     (((1,), (1,)), ((), ())),
                     preferred_element_type=jnp.float32,
                 )
-                s_ref[i, t] = s
-                new.append(jnp.maximum(best[i], lane_fold(s, jnp.maximum)))
+                s_ref[n, t] = s
+                new.append(jnp.maximum(best[n], lane_fold(s, jnp.maximum)))
             return tuple(new)
 
         low = jnp.full((BLOCK, 128), LOWEST, jnp.float32)
-        best = lax.fori_loop(0, groups, first, (low, low))
-
-        @pl.when(groups > 0)
-        def _():
-            key = lax.broadcasted_iota(jnp.int32, (BLOCK, width), 1)
-            for i in range(2):
-                valid = (counts[i] - (groups - 1) * GROUP) * BLOCK
-                s_ref[i, groups - 1] = jnp.where(key < valid, s_ref[i, groups - 1], LOWEST)
+        best = lax.fori_loop(0, groups, first, (low,) * len(chains))
+
+        key = lax.broadcasted_iota(jnp.int32, (BLOCK, width), 1)
+        for n in range(len(chains)):
+
+            def hide(t, carry, n=n):
+                s_ref[n, t] = jnp.where(key < (counts[n] - t * GROUP) * BLOCK, s_ref[n, t], LOWEST)
+                return carry
+
+            lax.fori_loop(lax.div(counts[n], GROUP), groups, hide, 0)
 
         top = [jnp.max(b, axis=1, keepdims=True) for b in best]
 
         def second(t, state):
             new = []
-            for i in range(2):
-                total, acc = state[i]
-                p = jnp.exp2((s_ref[i, t] - top[i]) * factor)
+            for n in range(len(chains)):
+                total, acc = state[n]
+                p = jnp.exp2((s_ref[n, t] - top[n]) * factor)
                 total = total + lane_fold(p, jnp.add)
                 acc = acc + jnp.dot(
-                    p.astype(jnp.bfloat16), gathered(v_ref, i, t), preferred_element_type=jnp.float32
+                    p.astype(jnp.bfloat16), gathered(v_ref, n, t), preferred_element_type=jnp.float32
                 )
                 new.append((total, acc))
             return tuple(new)
 
         zero = jnp.zeros((BLOCK, 128), jnp.float32)
-        state = lax.fori_loop(0, groups, second, ((zero, zero), (zero, zero)))
+        state = lax.fori_loop(0, groups, second, ((zero, zero),) * len(chains))
         lse = []
-        for i in range(2):
-            total = jnp.sum(state[i][0], axis=1, keepdims=True)
+        for n, (_, i) in enumerate(chains):
+            total = jnp.sum(state[n][0], axis=1, keepdims=True)
             some = total > 0.0
             safe = jnp.where(some, total, 1.0)
-            o_ref[c, hh, i * BLOCK : (i + 1) * BLOCK, :] = (state[i][1] / safe).astype(o_ref.dtype)
-            lse.append(jnp.where(some, top[i] * factor + jnp.log2(safe), LOWEST))
-        lse_ref[c, 0, pl.ds(hh, 1), :] = to_row(jnp.concatenate(lse, axis=0))
+            part = (state[n][1] / safe).astype(o_ref.dtype)
+            o_ref[c, hh[n], i * BLOCK : (i + 1) * BLOCK, :] = part
+            lse.append(jnp.where(some, top[n] * factor + jnp.log2(safe), LOWEST))
+        for a in range(bundle):
+            row = to_row(jnp.concatenate(lse[2 * a : 2 * a + 2], axis=0))
+            lse_ref[c, 0, pl.ds(first_head + a, 1), :] = row
         return carry
 
-    lax.fori_loop(0, heads * owners, one_pair, 0)
-
-
-def slash_attention(base, sorted_offsets, lo, hi, queries, keys, values, factor):
+    lax.fori_loop(0, heads // bundle * owners, one_bundle, 0)
+
+
+def slash_attention(lists, counts, queries, keys, values, factor):
     owners, head_count, rows, hd = queries.shape
     kv_heads, key_rows, _ = keys.shape
     heads = head_count // kv_heads
-    most = -(-sorted_offsets.shape[1] // GROUP)
+    length = lists.shape[-1]
+    most = length // GROUP
     elements = head_count * rows * owners * 48 * BLOCK
     return pl.pallas_call(
-        functools.partial(slash_kernel, factor, heads),
+        functools.partial(slash_kernel, factor, heads, length),
         grid_spec=pltpu.PrefetchScalarGridSpec(
-            num_scalar_prefetch=4,
+            num_scalar_prefetch=2,
             grid=(kv_heads,),
             in_specs=[
                 pl.BlockSpec((owners, heads, rows, hd), lambda g, *_: (0, g, 0, 0)),
@@ -126,7 +131,7 @@
                 pl.BlockSpec((owners, heads, rows, hd), lambda g, *_: (0, g, 0, 0)),
                 pl.BlockSpec((owners, 1, heads, rows), lambda g, *_: (0, g, 0, 0)),
             ],
-            scratch_shapes=[pltpu.VMEM((2, most, BLOCK, GROUP * BLOCK), jnp.float32)],
+            scratch_shapes=[pltpu.VMEM((2 * min(BUNDLE, heads), most, BLOCK, GROUP * BLOCK), jnp.float32)],
         ),
         out_shape=[
             jax.ShapeDtypeStruct(queries.shape, jnp.bfloat16),
@@ -136,7 +141,7 @@
         cost_estimate=pl.CostEstimate(
             flops=4 * elements * hd, bytes_accessed=12 * 2**20, transcendentals=elements
         ),
-    )(base, sorted_offsets, lo, hi, queries, keys, values)
+    )(lists.reshape(-1), counts.reshape(-1), queries, keys, values)
 
 
 def local_kernel(factor, me_ref, q_ref, kv_ref, vv_ref, kn_ref, vn_ref, bias_ref, o_ref, lse_ref):
@@ -287,6 +292,68 @@
     )(o, lse)
 
 
+def spread_kernel(y_ref, got_ref, send, recv):
+    size = lax.axis_size("kvh")
+    me = lax.axis_index("kvh")
+    ctx = lax.axis_index("ctx")
+    barrier = pltpu.get_barrier_semaphore()
+    for step in range(1, size):
+        to = lax.rem(me + step, size)
+        pl.semaphore_signal(barrier, inc=1, device_id=(ctx, to), device_id_type=MESH)
+    pl.semaphore_wait(barrier, size - 1)
+    copies = []
+    for step in range(1, size):
+        to = lax.rem(me + step, size)
+        copies.append(
+            pltpu.make_async_remote_copy(
+                src_ref=y_ref.at[to],
+                dst_ref=got_ref.at[step - 1],
+                send_sem=send.at[step - 1],
+                recv_sem=recv.at[step - 1],
+                device_id=(ctx, to),
+                device_id_type=MESH,
+            )
+        )
+    for copy in copies:
+        copy.start()
+    for copy in copies:
+        copy.wait()
+
+
+def sum_over_kvh(y):
+    size = lax.axis_size("kvh")
+    y = y.reshape(size, y.shape[0] // size, y.shape[1])
+    got = pl.pallas_call(
+        spread_kernel,
+        out_shape=jax.ShapeDtypeStruct((size - 1,) + y.shape[1:], y.dtype),
+        in_specs=[pl.BlockSpec(memory_space=pl.ANY)],
+        out_specs=pl.BlockSpec(memory_space=pl.ANY),
+        scratch_shapes=[
+            pltpu.SemaphoreType.DMA((size - 1,)),
+            pltpu.SemaphoreType.DMA((size - 1,)),
+        ],
+        compiler_params=pltpu.CompilerParams(collective_id=1, has_side_effects=True),
+    )(y)
+    own = lax.dynamic_index_in_dim(y, lax.axis_index("kvh"), axis=0, keepdims=False)
+    total = own.astype(jnp.float32) + jnp.sum(got.astype(jnp.float32), axis=0)
+    return total.astype(y.dtype)
+
+
+def block_lists(offsets, block_ids, base, blocks_dev):
+    diagonals = offsets.shape[1]
+    length = -(-diagonals // GROUP) * GROUP
+    rank = jnp.sum((offsets[:, :, None] > offsets[:, None, :]).astype(jnp.int32), axis=2)
+    found = base + block_ids[None, :, None] - offsets[:, None, :]
+    inside = (found >= 0) & (found < blocks_dev)
+    counts = jnp.sum(inside.astype(jnp.int32), axis=2)
+    below = jnp.sum((found >= blocks_dev).astype(jnp.int32), axis=2)
+    place = jnp.arange(length, dtype=jnp.int32)
+    place = below[:, :, None] + jnp.minimum(place[None, None, :], counts[:, :, None] - 1)
+    chosen = inside[:, :, None, :] & (rank[:, None, None, :] == place[:, :, :, None])
+    lists = jnp.sum(jnp.where(chosen, found[:, :, None, :] * BLOCK, 0), axis=3)
+    return lists, counts
+
+
 def slots_of(verticals, lower_block, blocks_dev):
     inside = (verticals >= lower_block) & (verticals < lower_block + blocks_dev)
     counts = inside.astype(jnp.int32)
@@ -327,23 +394,11 @@
     packed = jnp.concatenate([slot_keys, slot_values, fresh_keys, fresh_values], axis=0)
     gathered = lax.all_gather(packed, "ctx", axis=0, tiled=False)
 
-    rank = jnp.sum((offsets[:, :, None] > offsets[:, None, :]).astype(jnp.int32), axis=2)
-    places = jnp.arange(offsets.shape[1], dtype=jnp.int32)
-    sorted_offsets = jnp.sum(
-        jnp.where(rank[:, :, None] == places[None, None, :], offsets[:, :, None], 0), axis=1
-    )
     holder = me - (size - holders)
-    base = SPAN - holder * blocks_dev
     block_ids = jnp.arange(size * own_blocks, dtype=jnp.int32)
-    highest = (base + block_ids)[None, :, None]
-    hi = jnp.sum((offsets[:, None, :] <= highest).astype(jnp.int32), axis=2)
-    lo = jnp.sum((offsets[:, None, :] <= highest - blocks_dev).astype(jnp.int32), axis=2)
-    is_holder = holder >= 0
-    lo = jnp.where(is_holder, lo, 0)
-    hi = jnp.where(is_holder, hi, 0)
-    slash_o, slash_lse = slash_attention(
-        base.reshape(1), sorted_offsets, lo, hi, q_all, keys, values, factor
-    )
+    lists, counts = block_lists(offsets, block_ids, SPAN - holder * blocks_dev, blocks_dev)
+    counts = jnp.where(holder >= 0, counts, 0)
+    slash_o, slash_lse = slash_attention(lists, counts, q_all, keys, values, factor)
     part_o, part_lse = return_parts(slash_o, slash_lse, holders)
 
     own_ids = me * own_blocks + jnp.arange(own_blocks, dtype=jnp.int32)
@@ -368,11 +423,8 @@
         part_o.astype(jnp.float32) * (part_share / whole[None])[..., None], axis=0
     )
     attended = jnp.transpose(mixed.astype(jnp.bfloat16), (1, 0, 2)).reshape(own_rows, head_count * hd)
-    return lax.psum_scatter(
-        jnp.dot(attended, out_weight, preferred_element_type=jnp.float32).astype(jnp.bfloat16),
-        "kvh",
-        scatter_dimension=0,
-        tiled=True,
+    return sum_over_kvh(
+        jnp.dot(attended, out_weight, preferred_element_type=jnp.float32).astype(jnp.bfloat16)
     )
 
 

time: 381 us -> 253 us (0.66)
  Pallas kernels: 284 us -> 175 us
  waiting for transfers between devices: 48 us -> 20.3 us
  other arithmetic: 13.2 us -> 19.1 us
    pallas_call x1, Pallas kernels: 248 us -> 133 us  [return_parts(): pl.pallas_call(functools.partial(return_kernel, holders), out_shape=[jax....]
    reduce_scatter x1 -> x0, waiting for transfers between devices: 23.6 us -> none  [shards(): lax.psum_scatter(jnp.dot(attended, out_weight, preferred_element_type=jnp...]
    pallas_call x1 -> x2, Pallas kernels: 26.5 us -> 32.3 us  [the longest x1 17.7 us: sum_over_kvh(): pl.pallas_call(spread_kernel, out_shape=jax.ShapeDtypeStruct((size - 1,)...]
    reduce_sum x3 -> x4, other arithmetic: 1.63 us -> 6.8 us  [the longest x1 4.74 us: block_lists(): lists = jnp.sum(jnp.where(chosen, found[:, :, None, :] * BLOCK, 0), axis=3)]
    all_gather x1, waiting for transfers between devices: 24.4 us -> 20.2 us  [shards(): q_all = lax.all_gather(q_own, 'ctx', axis=0, tiled=False)]
  transfers between devices with their start and end apart: 3 -> 2, of which waited for: 2 -> 1; matrix products, arithmetic and copies ran while one was open for 7% -> 12% of each run, Pallas kernels for 72% -> 58%
where the time goes in v2:
time: 253 us
  Pallas kernels  175 us (69%)
  waiting for transfers between devices  20.3 us (8%)
  local copies, waits for them, and re-layouts  19.2 us (8%)
  other arithmetic  19.1 us (8%)
  between operations  13.7 us (5%)
  matrix products  5.66 us (2%)
    pallas_call x1, Pallas kernels, return_parts(): pl.pallas_call(functools.partial(return_kernel, holders), out_shape=[jax....  133 us
    all_gather x1, waiting for transfers between devices, shards(): q_all = lax.all_gather(q_own, 'ctx', axis=0, tiled=False)  20.2 us
    pallas_call x1, Pallas kernels, sum_over_kvh(): pl.pallas_call(spread_kernel, out_shape=jax.ShapeDtypeStruct((size - 1,)...  17.7 us
    pallas_call x1, Pallas kernels, slash_attention(): pl.pallas_call(functools.partial(slash_kernel, factor, heads, length), gr...  14.6 us
    unnamed x14, local copies, waits for them, and re-layouts  11 us
    pallas_call x1, Pallas kernels, local_attention(): pl.pallas_call(functools.partial(local_kernel, factor), grid_spec=pltpu.P...  9.27 us
    dot_general x1, matrix products, shards(): jnp.dot(attended, out_weight, preferred_element_type=jnp.float32)  5.66 us
  transfers between devices with their start and end apart: 2, of which 1 were waited for; matrix products, arithmetic and copies ran while one was open for 12% of the time, Pallas kernels for 58%

profile of v2, /device:TPU:21, one launch (start us, length us, event | category | flops | bytes accessed | tf_op | source)
XLA Modules:
  0.0 252.5 jit_solution(5548607814782913214)
XLA Ops:
  6.5 1.7 copy.48
  8.3 0.7 fusion.26
  9.0 0.2 reduce_window_sum.55
  9.2 0.2 reduce_window_sum.51
  9.4 0.2 reduce_window_sum.50
  10.8 1.1 select_reduce_fusion.1
  12.1 9.2 %fusion.35 = (bf16[8192,2,128]{2,0,1:T(8,128)(2,1)}, bf16[2,8192,128]{2,1,0:T(8,128)(2,1)}, bf16[2,8192,128]{2,1,0:T(8,128)(2,1)}, bf16[8192,2,128]{2,0,1:T(8,128)(2,1)}) fusion(bf16[8192,2,128]{2,1,0:T(2,128)(2,1)} %param.11, bf16[8192,2,128]{2,1,0:T(2,128)(2,1)} %param.12), kind=kLoop, calls=%fused_computation.120 | loop fusion | bytes 25165824 | tf_op args[3]
  21.3 2.8 %gather_fusion = bf16[16,64,128]{2,1,0:T(8,128)(2,1)S(1)} fusion(bf16[256,64,128]{2,1,0:T(8,128)(2,1)} %bitcast.65, s32[1024]{0:T(1024)S(1)} %pad_clamp_fusion), kind=kCustom, calls=%fused_computation | custom fusion | bytes 524352 | tf_op jit(solution)/shard_map/gather | solution.py:390
  24.1 2.8 %gather_fusion.1 = bf16[16,64,128]{2,1,0:T(8,128)(2,1)S(1)} fusion(bf16[256,64,128]{2,1,0:T(8,128)(2,1)} %bitcast.64, s32[1024]{0:T(1024)S(1)} %pad_clamp_fusion), kind=kCustom, calls=%fused_computation.1 | custom fusion | bytes 524352 | tf_op jit(solution)/shard_map/gather | solution.py:391
  27.0 0.9 pad_maximum_fusion
  28.9 0.7 compare_reduce_fusion.1
  29.8 0.8 reshape.361.bias_ref
  30.6 0.3 convert_reduce_fusion.1
  30.9 0.4 convert_reduce_fusion.3
  31.6 4.7 %select_reduce_fusion = s32[8,16,96]{2,1,0:T(8,128)S(1)} fusion(s32[8,16,96]{2,1,0:T(8,128)S(1)} %get-tuple-element.54, s32[8,16,96]{2,1,0:T(8,128)S(1)} %minimum_add_fusion, s32[8,96]{1,0:T(8,128)S(1)} %convert_reduce_fusion.1, pred[8,16,96]{2,1,0:T(8,128)(4,1)S(1)} %fusion.2), kind=kLoop, calls=%fused_computation.2 | loop fusion | flops 4706304 | bytes 162816 | tf_op jit(solution)/shard_map/reduce_sum | solution.py:353
  36.3 0.7 reshape.363.list_ref
  37.0 0.6 select_n.234.count_ref
  37.6 20.2 %all-gather.7.cloned.1.call-done = bf16[64,128,128]{2,1,0:T(8,128)(2,1)} async-done(((bf16[8,128,128]{2,1,0:T(8,128)(2,1)}), bf16[64,128,128]{2,1,0:T(8,128)(2,1)}) %all-gather.7.cloned.1.call-update) | async-done | bytes 2097168 | tf_op jit(solution)/shard_map/all_gather | solution.py:382
  57.9 14.6 %shard_map.83 = (bf16[8,8,128,128]{3,2,1,0:T(8,128)(2,1)}, f32[8,2,4,128]{3,2,1,0:T(4,128)}) custom-call(s32[12288]{0:T(1024)} %reshape.363.list_ref, s32[128]{0:T(128)} %select_n.234.count_ref, bf16[8,8,128,128]{3,2,1,0:T(8,128)(2,1)} %bitcast.80, bf16[2,8192,128]{2,1,0:T(8,128)(2,1)} %get-tuple-element.51.k_ref, bf16[2,8192,128]{2,1,0:T(8,128)(2,1)} %get-tuple-element.73.v_ref), custom_call_target="tpu_custom_call" | custom-call | flops 12884901888 | bytes 12582912 | tf_op jit(solution)/shard_map/pallas_call | solution.py:120
  72.5 133.0 %shard_map.84 = (bf16[2,8,128,128]{3,2,1,0:T(8,128)(2,1)}, f32[2,2,4,128]{3,2,1,0:T(4,128)}) custom-call(bf16[8,8,128,128]{3,2,1,0:T(8,128)(2,1)} %get-tuple-element.13.o_ref, f32[8,2,4,128]{3,2,1,0:T(4,128)} %get-tuple-element.14.l_ref), custom_call_target="tpu_custom_call" | custom-call | tf_op jit(solution)/shard_map/pallas_call | solution.py:275
  205.4 0.7 reduce_max.11
  206.2 9.3 %shard_map.82 = (f32[8,128,128]{2,1,0:T(8,128)}, f32[8,1,128]{2,1,0:T(1,128)}) custom-call(s32[1]{0:T(128)} %bitcast.me_ref, bf16[8,128,128]{2,1,0:T(8,128)(2,1)} %bitcast.67, bf16[8,40,64,128]{3,2,1,0:T(8,128)(2,1)} %bitcast.58, bf16[8,40,64,128]{3,2,1,0:T(8,128)(2,1)} %bitcast.59, bf16[8,40,64,128]{3,2,1,0:T(8,128)(2,1)} %bitcast.60, ...), custom_call_target="tpu_custom_call" | custom-call | flops 1073741824 | bytes 6291456 | tf_op jit(solution)/shard_map/pallas_call | solution.py:187
  215.4 0.7 max.18
  216.1 0.7 fusion.21
  216.8 0.7 fusion.22
  217.6 0.3 multiply_reduce_fusion
  217.9 1.2 fusion.1
  219.2 0.2 copy.42
  219.3 5.7 %convolution_convert_fusion = bf16[128,4096]{1,0:T(8,128)(2,1)} fusion(bf16[128,1024]{0,1:T(8,128)(2,1)S(1)} %bitcast.68, bf16[1024,4096]{1,0:T(8,128)(2,1)} %param.15), kind=kOutput, calls=%fused_computation.3 | convolution fusion | flops 1074266112 | bytes 9699328 | tf_op jit(solution)/shard_map/dot_general | solution.py:427
  225.0 17.7 %shard_map.85 = bf16[3,32,4096]{2,1,0:T(8,128)(2,1)} custom-call(bf16[4,32,4096]{2,1,0:T(8,128)(2,1)} %bitcast.62), custom_call_target="tpu_custom_call" | custom-call | tf_op jit(solution)/shard_map/pallas_call | solution.py:326
  242.7 1.3 convert_reduce_fusion
  244.0 1.7 fusion
  (66 shorter events, 2.7 us)
Async XLA Ops:
  6.5 51.3 %all-gather.7.cloned.1.call-start = ((), (), s32[]{:S(2)}) async-start(), calls=%async_computation.1 | async-start | bytes 2359296 | tf_op jit(solution)/shard_map/all_gather | solution.py:382
  8.2 197.9 %all-gather.5.cloned.1.call-start = ((), (), s32[]{:S(2)}) async-start(), calls=%async_computation | async-start | bytes 5898240 | tf_op jit(solution)/shard_map/all_gather | solution.py:395
  12.0 14.9 %copy-start.3 = (bf16[128,2,128]{2,1,0:T(2,128)(2,1)S(1)}, bf16[128,2,128]{2,1,0:T(2,128)(2,1)}, u32[]{:S(2)}) copy-start(bf16[128,2,128]{2,1,0:T(2,128)(2,1)} %param.10) | copy-start | bytes 196612
  12.1 14.9 %copy-start.4 = (bf16[128,2,128]{2,1,0:T(2,128)(2,1)S(1)}, bf16[128,2,128]{2,1,0:T(2,128)(2,1)}, u32[]{:S(2)}) copy-start(bf16[128,2,128]{2,1,0:T(2,128)(2,1)} %param.9) | copy-start | bytes 196612
  12.1 16.7 %copy-start.1 = (s32[8,96]{1,0:T(8,128)S(1)}, s32[8,96]{1,0:T(8,128)}, u32[]{:S(2)}) copy-start(s32[8,96]{1,0:T(8,128)} %param.14) | copy-start | bytes 9220
  206.2 10.0 %copy-start.2 = (f32[2,2,4,128]{3,2,1,0:T(4,128)S(1)}, f32[2,2,4,128]{3,2,1,0:T(4,128)}, u32[]{:S(2)}) copy-start(f32[2,2,4,128]{3,2,1,0:T(4,128)} %get-tuple-element.15) | copy-start | bytes 24580
  206.2 11.4 %copy-start = (bf16[2,8,128,128]{3,2,1,0:T(8,128)(2,1)S(1)}, bf16[2,8,128,128]{3,2,1,0:T(8,128)(2,1)}, u32[]{:S(2)}) copy-start(bf16[2,8,128,128]{3,2,1,0:T(8,128)(2,1)} %get-tuple-element.16) | copy-start | bytes 1572868
Sparse Core Ops, SparseCore 0:
  9.5 48.3 all-gather.6
  60.1 84.5 all-gather.4

commit v3 on v2

--- a/solution.py
+++ b/solution.py
@@ -144,7 +144,7 @@
     )(lists.reshape(-1), counts.reshape(-1), queries, keys, values)
 
 
-def local_kernel(factor, me_ref, q_ref, kv_ref, vv_ref, kn_ref, vn_ref, bias_ref, o_ref, lse_ref):
+def local_head(factor, q_ref, kv_ref, vv_ref, kn_ref, vn_ref, bias_ref, o_ref, lse_ref):
     rows, hd = q_ref.shape[1:]
     blocks = rows // BLOCK
 
@@ -162,7 +162,7 @@
     s_vert = scores(flat(kv_ref), 0)
     s_new = scores(flat(kn_ref), 1)
     key = lax.broadcasted_iota(jnp.int32, s_new.shape, 1)
-    row = lax.broadcasted_iota(jnp.int32, s_new.shape, 0) + me_ref[0] * rows
+    row = lax.broadcasted_iota(jnp.int32, s_new.shape, 0) + lax.axis_index("ctx") * rows
     s_new = jnp.where(key <= row, s_new, LOWEST)
     top = jnp.maximum(
         jnp.max(lane_fold(s_vert, jnp.maximum), axis=1, keepdims=True),
@@ -178,54 +178,16 @@
     lse_ref[0] = to_row(top * factor + jnp.log2(total))
 
 
-def local_attention(me, queries, gathered, bias, kv_heads, factor):
-    head_count, rows, hd = queries.shape
-    owners = gathered.shape[0]
-    blocks = rows // BLOCK
-    group = head_count // kv_heads
-    piece = (owners, 2, BLOCK, hd)
-    return pl.pallas_call(
-        functools.partial(local_kernel, factor),
-        grid_spec=pltpu.PrefetchScalarGridSpec(
-            num_scalar_prefetch=1,
-            grid=(head_count,),
-            in_specs=[
-                pl.BlockSpec((1, rows, hd), lambda h, *_: (h, 0, 0)),
-                pl.BlockSpec(piece, lambda h, *_: (0, h, 0, 0)),
-                pl.BlockSpec(piece, lambda h, *_: (0, head_count + h, 0, 0)),
-                pl.BlockSpec(piece, lambda h, *_: (0, 2 * head_count + h // group, 0, 0)),
-                pl.BlockSpec(piece, lambda h, *_: (0, 2 * head_count + kv_heads + h // group, 0, 0)),
-                pl.BlockSpec((1, 2, blocks, bias.shape[-1]), lambda h, *_: (h, 0, 0, 0)),
-            ],
-            out_specs=[
-                pl.BlockSpec((1, rows, hd), lambda h, *_: (h, 0, 0)),
-                pl.BlockSpec((1, 1, rows), lambda h, *_: (h, 0, 0)),
-            ],
-        ),
-        out_shape=[
-            jax.ShapeDtypeStruct(queries.shape, jnp.float32),
-            jax.ShapeDtypeStruct((head_count, 1, rows), jnp.float32),
-        ],
-        compiler_params=pltpu.CompilerParams(vmem_limit_bytes=VMEM_LIMIT),
-        cost_estimate=pl.CostEstimate(
-            flops=4 * head_count * rows * hd * 2 * bias.shape[-1],
-            bytes_accessed=6 * 2**20,
-            transcendentals=head_count * rows * 2 * bias.shape[-1],
-        ),
-    )(me, queries, gathered, gathered, gathered, gathered, bias)
-
-
-def return_kernel(holders, o_ref, l_ref, part_ref, plse_ref, o_send, l_send, o_recv, l_recv, o_own, l_own):
+def local_kernel(
+    factor, holders, q_ref, kv_ref, vv_ref, kn_ref, vn_ref, bias_ref, o_ref, l_ref,
+    own_ref, own_lse_ref, part_ref, plse_ref, o_send, l_send, o_recv, l_recv, o_own, l_own,
+):
     size = lax.axis_size("ctx")
     me = lax.axis_index("ctx")
     kvh = lax.axis_index("kvh")
     first = size - holders
-    barrier = pltpu.get_barrier_semaphore()
-    for r in range(holders):
-
-        @pl.when(me != first + r)
-        def _():
-            pl.semaphore_signal(barrier, inc=1, device_id=(first + r, kvh), device_id_type=MESH)
+    turn = pl.program_id(0)
+    last = pl.num_programs(0) - 1
 
     def copies(r, step):
         to = lax.rem(me + step, size)
@@ -242,54 +204,95 @@
             for src, dst, send, recv in pairs
         ]
 
-    for r in range(holders):
-
-        @pl.when(me == first + r)
-        def _():
-            pl.semaphore_wait(barrier, size - 1)
-            for step in range(1, size):
-                for copy in copies(r, step):
+    def own_copies(r):
+        return [
+            pltpu.make_async_copy(o_ref.at[me], part_ref.at[r], o_own),
+            pltpu.make_async_copy(l_ref.at[me], plse_ref.at[r], l_own),
+        ]
+
+    @pl.when(turn == 0)
+    def _():
+        barrier = pltpu.get_barrier_semaphore()
+        for r in range(holders):
+
+            @pl.when(me != first + r)
+            def _():
+                pl.semaphore_signal(barrier, inc=1, device_id=(first + r, kvh), device_id_type=MESH)
+
+        for r in range(holders):
+
+            @pl.when(me == first + r)
+            def _():
+                pl.semaphore_wait(barrier, size - 1)
+                for step in range(1, size):
+                    for copy in copies(r, step):
+                        copy.start()
+                for copy in own_copies(r):
                     copy.start()
-            own = [
-                pltpu.make_async_copy(o_ref.at[me], part_ref.at[r], o_own),
-                pltpu.make_async_copy(l_ref.at[me], plse_ref.at[r], l_own),
-            ]
-            for copy in own:
-                copy.start()
-            for copy in own:
-                copy.wait()
-            for step in range(1, size):
-                for copy in copies(r, step):
-                    copy.wait_send()
-
-    for r in range(holders):
-
-        @pl.when(me != first + r)
-        def _():
-            for copy in copies(r, 1):
-                copy.wait_recv()
-
-
-def return_parts(o, lse, holders):
-    size = o.shape[0]
+
+    local_head(factor, q_ref, kv_ref, vv_ref, kn_ref, vn_ref, bias_ref, own_ref, own_lse_ref)
+
+    @pl.when(turn == last)
+    def _():
+        for r in range(holders):
+
+            @pl.when(me == first + r)
+            def _():
+                for copy in own_copies(r):
+                    copy.wait()
+                for step in range(1, size):
+                    for copy in copies(r, step):
+                        copy.wait_send()
+
+            @pl.when(me != first + r)
+            def _():
+                for copy in copies(r, 1):
+                    copy.wait_recv()
+
+
+def local_attention(queries, gathered, bias, kv_heads, factor, slash_o, slash_lse, holders):
+    head_count, rows, hd = queries.shape
+    owners = gathered.shape[0]
+    blocks = rows // BLOCK
+    group = head_count // kv_heads
+    piece = (owners, 2, BLOCK, hd)
     return pl.pallas_call(
-        functools.partial(return_kernel, holders),
+        functools.partial(local_kernel, factor, holders),
+        grid=(head_count,),
+        in_specs=[
+            pl.BlockSpec((1, rows, hd), lambda h: (h, 0, 0)),
+            pl.BlockSpec(piece, lambda h: (0, h, 0, 0)),
+            pl.BlockSpec(piece, lambda h: (0, head_count + h, 0, 0)),
+            pl.BlockSpec(piece, lambda h: (0, 2 * head_count + h // group, 0, 0)),
+            pl.BlockSpec(piece, lambda h: (0, 2 * head_count + kv_heads + h // group, 0, 0)),
+            pl.BlockSpec((1, 2, blocks, bias.shape[-1]), lambda h: (h, 0, 0, 0)),
+            pl.BlockSpec(memory_space=pl.ANY),
+            pl.BlockSpec(memory_space=pl.ANY),
+        ],
+        out_specs=[
+            pl.BlockSpec((1, rows, hd), lambda h: (h, 0, 0)),
+            pl.BlockSpec((1, 1, rows), lambda h: (h, 0, 0)),
+            pl.BlockSpec(memory_space=pl.ANY),
+            pl.BlockSpec(memory_space=pl.ANY),
+        ],
         out_shape=[
-            jax.ShapeDtypeStruct((holders,) + o.shape[1:], o.dtype),
-            jax.ShapeDtypeStruct((holders,) + lse.shape[1:], lse.dtype),
-        ],
-        in_specs=[pl.BlockSpec(memory_space=pl.ANY)] * 2,
-        out_specs=[pl.BlockSpec(memory_space=pl.ANY)] * 2,
+            jax.ShapeDtypeStruct(queries.shape, jnp.float32),
+            jax.ShapeDtypeStruct((head_count, 1, rows), jnp.float32),
+            jax.ShapeDtypeStruct((holders,) + slash_o.shape[1:], slash_o.dtype),
+            jax.ShapeDtypeStruct((holders,) + slash_lse.shape[1:], slash_lse.dtype),
+        ],
         scratch_shapes=[
-            pltpu.SemaphoreType.DMA((size - 1,)),
-            pltpu.SemaphoreType.DMA((size - 1,)),
+            pltpu.SemaphoreType.DMA((owners - 1,)),
+            pltpu.SemaphoreType.DMA((owners - 1,)),
             pltpu.SemaphoreType.DMA((holders,)),
             pltpu.SemaphoreType.DMA((holders,)),
             pltpu.SemaphoreType.DMA,
             pltpu.SemaphoreType.DMA,
         ],
-        compiler_params=pltpu.CompilerParams(collective_id=0, has_side_effects=True),
-    )(o, lse)
+        compiler_params=pltpu.CompilerParams(
+            collective_id=0, has_side_effects=True, vmem_limit_bytes=VMEM_LIMIT
+        ),
+    )(queries, gathered, gathered, gathered, gathered, bias, slash_o, slash_lse)
 
 
 def spread_kernel(y_ref, got_ref, send, recv):
@@ -399,7 +402,6 @@
     lists, counts = block_lists(offsets, block_ids, SPAN - holder * blocks_dev, blocks_dev)
     counts = jnp.where(holder >= 0, counts, 0)
     slash_o, slash_lse = slash_attention(lists, counts, q_all, keys, values, factor)
-    part_o, part_lse = return_parts(slash_o, slash_lse, holders)
 
     own_ids = me * own_blocks + jnp.arange(own_blocks, dtype=jnp.int32)
     slots = jnp.stack([slots_of(verticals, c * blocks_dev, blocks_dev) for c in range(size)], axis=1)
@@ -411,7 +413,9 @@
     new_ok = jnp.any(new_ids[None, None, :, None] == slash_blocks[:, :, None, :], axis=-1)
     bias = jnp.where(jnp.stack([vert_ok, new_ok], axis=1), 0.0, LOWEST).astype(jnp.float32)
     bias = jnp.repeat(bias, BLOCK, axis=-1)
-    own_o, own_lse = local_attention(me.reshape(1), q_own, gathered, bias, kv_heads, factor)
+    own_o, own_lse, part_o, part_lse = local_attention(
+        q_own, gathered, bias, kv_heads, factor, slash_o, slash_lse, holders
+    )
 
     own_lse = own_lse.reshape(head_count, own_rows)
     part_lse = part_lse.reshape(holders, head_count, own_rows)

time: 253 us -> 248 us (0.980)
  Pallas kernels: 175 us -> 94.6 us
  waiting for transfers between devices: 20.3 us -> 92.5 us
    pallas_call x2 -> x1, Pallas kernels: 142 us -> 64.1 us  [local_attention(): pl.pallas_call(functools.partial(local_kernel, factor, holders), grid=(he...]
    all_gather x1, waiting for transfers between devices: 0.01 us -> 72.3 us  [shards(): gathered = lax.all_gather(packed, 'ctx', axis=0, tiled=False)]
    unnamed x14 -> x9, local copies, waits for them, and re-layouts: 11 us -> 1.73 us
    transpose x0 -> x1, local copies, waits for them, and re-layouts: none -> 9.25 us  [shards(): values = jnp.transpose(cache_values, (1, 0, 2))]
  transfers between devices with their start and end apart: 2 -> 2, of which waited for: 1 -> 2; matrix products, arithmetic and copies ran while one was open for 12% -> 12% of each run, Pallas kernels for 58% -> 6%
where the time goes in v3:
time: 248 us; the launch traced here: 247 us
  Pallas kernels  94.6 us (38%)
  waiting for transfers between devices  92.5 us (37%)
  other arithmetic  21.5 us (9%)
  local copies, waits for them, and re-layouts  19.2 us (8%)
  between operations  13.7 us (6%)
  matrix products  5.66 us (2%)
    all_gather x1, waiting for transfers between devices, shards(): gathered = lax.all_gather(packed, 'ctx', axis=0, tiled=False)  72.3 us
    pallas_call x1, Pallas kernels, local_attention(): pl.pallas_call(functools.partial(local_kernel, factor, holders), grid=(he...  64.1 us
    all_gather x1, waiting for transfers between devices, shards(): q_all = lax.all_gather(q_own, 'ctx', axis=0, tiled=False)  20.2 us
    pallas_call x1, Pallas kernels, sum_over_kvh(): pl.pallas_call(spread_kernel, out_shape=jax.ShapeDtypeStruct((size - 1,)...  15.9 us
    pallas_call x1, Pallas kernels, slash_attention(): pl.pallas_call(functools.partial(slash_kernel, factor, heads, length), gr...  14.6 us
    transpose x1, local copies, waits for them, and re-layouts, shards(): values = jnp.transpose(cache_values, (1, 0, 2))  9.25 us
    dot_general x1, matrix products, shards(): jnp.dot(attended, out_weight, preferred_element_type=jnp.float32)  5.66 us
  transfers between devices with their start and end apart: 2, of which 2 were waited for; matrix products, arithmetic and copies ran while one was open for 12% of the time, Pallas kernels for 6%

profile of v3, /device:TPU:21, one launch (start us, length us, event | category | flops | bytes accessed | tf_op | source)
XLA Modules:
  0.0 247.3 jit_solution(285129902108130352)
XLA Ops:
  6.5 1.7 copy.48
  8.3 0.7 fusion.26
  9.0 0.2 reduce_window_sum.55
  10.8 1.1 select_reduce_fusion.1
  12.1 9.2 %copy_bitcast_fusion.1 = (bf16[2,8192,128]{2,1,0:T(8,128)(2,1)}, bf16[8192,2,128]{2,0,1:T(8,128)(2,1)}, bf16[8192,2,128]{2,0,1:T(8,128)(2,1)}, bf16[2,8192,128]{2,1,0:T(8,128)(2,1)}) fusion(bf16[8192,2,128]{2,1,0:T(2,128)(2,1)} %param.12, bf16[8192,2,128]{2,1,0:T(2,128)(2,1)} %param.11), kind=kLoop, calls=%fused_computation.109 | loop fusion | bytes 25165824 | tf_op jit(solution)/shard_map/transpose | solution.py:388
  21.3 2.8 %gather_fusion = bf16[16,64,128]{2,1,0:T(8,128)(2,1)S(1)} fusion(bf16[256,64,128]{2,1,0:T(8,128)(2,1)} %bitcast.64, s32[1024]{0:T(1024)S(1)} %pad_clamp_fusion), kind=kCustom, calls=%fused_computation | custom fusion | bytes 524352 | tf_op jit(solution)/shard_map/gather | solution.py:393
  24.1 2.8 %gather_fusion.1 = bf16[16,64,128]{2,1,0:T(8,128)(2,1)S(1)} fusion(bf16[256,64,128]{2,1,0:T(8,128)(2,1)} %bitcast.63, s32[1024]{0:T(1024)S(1)} %pad_clamp_fusion), kind=kCustom, calls=%fused_computation.1 | custom fusion | bytes 524352 | tf_op jit(solution)/shard_map/gather | solution.py:394
  27.0 0.9 pad_maximum_fusion
  28.9 0.7 compare_reduce_fusion.1
  29.8 0.8 reshape.357.bias_ref
  30.6 0.3 convert_reduce_fusion.1
  30.9 0.4 convert_reduce_fusion.3
  31.6 4.7 %select_reduce_fusion = s32[8,16,96]{2,1,0:T(8,128)S(1)} fusion(s32[8,16,96]{2,1,0:T(8,128)S(1)} %get-tuple-element.54, s32[8,16,96]{2,1,0:T(8,128)S(1)} %minimum_add_fusion, s32[8,96]{1,0:T(8,128)S(1)} %convert_reduce_fusion.1, pred[8,16,96]{2,1,0:T(8,128)(4,1)S(1)} %fusion.2), kind=kLoop, calls=%fused_computation.2 | loop fusion | flops 4706304 | bytes 162816 | tf_op jit(solution)/shard_map/reduce_sum | solution.py:356
  36.3 0.7 reshape.358.list_ref
  37.0 0.6 select_n.234.count_ref
  37.6 20.2 %all-gather.7.cloned.1.call-done = bf16[64,128,128]{2,1,0:T(8,128)(2,1)} async-done(((bf16[8,128,128]{2,1,0:T(8,128)(2,1)}), bf16[64,128,128]{2,1,0:T(8,128)(2,1)}) %all-gather.7.cloned.1.call-update) | async-done | bytes 2097168 | tf_op jit(solution)/shard_map/all_gather | solution.py:385
  57.9 14.6 %shard_map.82 = (bf16[8,8,128,128]{3,2,1,0:T(8,128)(2,1)}, f32[8,2,4,128]{3,2,1,0:T(4,128)}) custom-call(s32[12288]{0:T(1024)} %reshape.358.list_ref, s32[128]{0:T(128)} %select_n.234.count_ref, bf16[8,8,128,128]{3,2,1,0:T(8,128)(2,1)} %bitcast.79, bf16[2,8192,128]{2,1,0:T(8,128)(2,1)} %get-tuple-element.82.k_ref, bf16[2,8192,128]{2,1,0:T(8,128)(2,1)} %get-tuple-element.50.v_ref), custom_call_target="tpu_custom_call" | custom-call | flops 12884901888 | bytes 12582912 | tf_op jit(solution)/shard_map/pallas_call | solution.py:120
  72.5 72.3 %all-gather.5.cloned.1.call-done = bf16[320,64,128]{2,1,0:T(8,128)(2,1)} async-done(((bf16[40,64,128]{2,1,0:T(8,128)(2,1)}), bf16[320,64,128]{2,1,0:T(8,128)(2,1)}) %all-gather.5.cloned.1.call-update) | async-done | bytes 5242896 | tf_op jit(solution)/shard_map/all_gather | solution.py:398
  144.7 64.1 %shard_map.83 = (f32[8,128,128]{2,1,0:T(8,128)}, f32[8,1,128]{2,1,0:T(1,128)}, bf16[2,8,128,128]{3,2,1,0:T(8,128)(2,1)}, f32[2,2,4,128]{3,2,1,0:T(4,128)}) custom-call(bf16[8,128,128]{2,1,0:T(8,128)(2,1)} %bitcast.66, bf16[8,40,64,128]{3,2,1,0:T(8,128)(2,1)} %bitcast.57, bf16[8,40,64,128]{3,2,1,0:T(8,128)(2,1)} %bitcast.58, ...), custom_call_target="tpu_custom_call" | custom-call | tf_op jit(solution)/shard_map/pallas_call | solution.py:259
  208.9 0.7 reduce_max.11
  209.6 0.7 max.18
  210.3 0.7 exponential_reduce_fusion
  211.0 0.7 fusion.21
  211.7 0.7 fusion.22
  212.4 0.7 exponential_divide_fusion
  213.1 1.4 multiply_reduce_fusion
  214.5 1.2 fusion.1
  215.7 0.2 copy.42
  215.9 5.7 %convolution_convert_fusion = bf16[128,4096]{1,0:T(8,128)(2,1)} fusion(bf16[128,1024]{0,1:T(8,128)(2,1)S(1)} %bitcast.67, bf16[1024,4096]{1,0:T(8,128)(2,1)} %param.15), kind=kOutput, calls=%fused_computation.3 | convolution fusion | flops 1074266112 | bytes 9699328 | tf_op jit(solution)/shard_map/dot_general | solution.py:431
  221.6 15.9 %shard_map.84 = bf16[3,32,4096]{2,1,0:T(8,128)(2,1)} custom-call(bf16[4,32,4096]{2,1,0:T(8,128)(2,1)} %bitcast.61), custom_call_target="tpu_custom_call" | custom-call | tf_op jit(solution)/shard_map/pallas_call | solution.py:329
  237.5 1.3 convert_reduce_fusion
  238.8 1.7 fusion
  (61 shorter events, 3.0 us)
Async XLA Ops:
  6.5 51.3 %all-gather.7.cloned.1.call-start = ((), (), s32[]{:S(2)}) async-start(), calls=%async_computation.1 | async-start | bytes 2359296 | tf_op jit(solution)/shard_map/all_gather | solution.py:385
  8.2 136.5 %all-gather.5.cloned.1.call-start = ((), (), s32[]{:S(2)}) async-start(), calls=%async_computation | async-start | bytes 5898240 | tf_op jit(solution)/shard_map/all_gather | solution.py:398
  12.0 14.9 %copy-start.1 = (bf16[128,2,128]{2,1,0:T(2,128)(2,1)S(1)}, bf16[128,2,128]{2,1,0:T(2,128)(2,1)}, u32[]{:S(2)}) copy-start(bf16[128,2,128]{2,1,0:T(2,128)(2,1)} %param.9) | copy-start | bytes 196612
  12.1 14.9 %copy-start.2 = (bf16[128,2,128]{2,1,0:T(2,128)(2,1)S(1)}, bf16[128,2,128]{2,1,0:T(2,128)(2,1)}, u32[]{:S(2)}) copy-start(bf16[128,2,128]{2,1,0:T(2,128)(2,1)} %param.10) | copy-start | bytes 196612
  12.1 16.7 %copy-start = (s32[8,96]{1,0:T(8,128)S(1)}, s32[8,96]{1,0:T(8,128)}, u32[]{:S(2)}) copy-start(s32[8,96]{1,0:T(8,128)} %param.14) | copy-start | bytes 9220
Sparse Core Ops, SparseCore 0:
  9.5 48.3 all-gather.6
  60.1 84.6 all-gather.4

commit v4 on v3

--- a/solution.py
+++ b/solution.py
@@ -382,7 +382,10 @@
     factor = math.log2(math.e) / math.sqrt(hd)
 
     q_own = jnp.transpose(queries, (1, 0, 2))
-    q_all = lax.all_gather(q_own, "ctx", axis=0, tiled=False)
+    q_all = [
+        lax.all_gather(q_own[g * group : (g + 1) * group], "ctx", axis=0, tiled=False)
+        for g in range(kv_heads)
+    ]
 
     keys = jnp.transpose(cache_keys, (1, 0, 2))
     values = jnp.transpose(cache_values, (1, 0, 2))
@@ -401,7 +404,19 @@
     block_ids = jnp.arange(size * own_blocks, dtype=jnp.int32)
     lists, counts = block_lists(offsets, block_ids, SPAN - holder * blocks_dev, blocks_dev)
     counts = jnp.where(holder >= 0, counts, 0)
-    slash_o, slash_lse = slash_attention(lists, counts, q_all, keys, values, factor)
+    parts = [
+        slash_attention(
+            lists[g * group : (g + 1) * group],
+            counts[g * group : (g + 1) * group],
+            q_all[g],
+            keys[g : g + 1],
+            values[g : g + 1],
+            factor,
+        )
+        for g in range(kv_heads)
+    ]
+    slash_o = jnp.concatenate([o for o, _ in parts], axis=1)
+    slash_lse = jnp.concatenate([lse for _, lse in parts], axis=1)
 
     own_ids = me * own_blocks + jnp.arange(own_blocks, dtype=jnp.int32)
     slots = jnp.stack([slots_of(verticals, c * blocks_dev, blocks_dev) for c in range(size)], axis=1)

time: 248 us -> 255 us (1.028)
  Pallas kernels: 94.6 us -> 73.5 us
  waiting for transfers between devices: 92.5 us -> 111 us
  local copies, waits for them, and re-layouts: 19.2 us -> 24.9 us
  other arithmetic: 21.5 us -> 25.7 us
    pallas_call x1, Pallas kernels: 64.1 us -> 38.5 us  [local_attention(): pl.pallas_call(functools.partial(local_kernel, factor, holders), grid=(he...]
    all_gather x1 -> x2, waiting for transfers between devices: 20.2 us -> 35.6 us  [shards(): lax.all_gather(q_own[g * group:(g + 1) * group], 'ctx', axis=0, tiled=False)]
    transpose x1 -> x0, local copies, waits for them, and re-layouts: 9.25 us -> none  [shards(): values = jnp.transpose(cache_values, (1, 0, 2))]
    unnamed x9 -> x19, local copies, waits for them, and re-layouts: 1.73 us -> 8.54 us
    slice x0 -> x4, local copies, waits for them, and re-layouts: none -> 6.81 us  [the longest x1 6.03 us: shards(): values[g:g + 1]]
    concatenate x0 -> x2, other arithmetic: none -> 4.17 us  [the longest x1 2.85 us: shards(): slash_o = jnp.concatenate([o for o, _ in parts], axis=1)]
    pallas_call x1 -> x2, Pallas kernels: 14.6 us -> 18.7 us  [slash_attention(): pl.pallas_call(functools.partial(slash_kernel, factor, heads, length), gr...]
  transfers between devices with their start and end apart: 2 -> 3, of which waited for: 2 -> 3; matrix products, arithmetic and copies ran while one was open for 12% -> 15% of each run, Pallas kernels for 6% -> 7%
where the time goes in v4:
time: 255 us; the launch traced here: 254 us
  waiting for transfers between devices  111 us (44%)
  Pallas kernels  73.5 us (29%)
  other arithmetic  25.7 us (10%)
  local copies, waits for them, and re-layouts  24.9 us (10%)
  between operations  13.4 us (5%)
  matrix products  5.66 us (2%)
    all_gather x1, waiting for transfers between devices, shards(): gathered = lax.all_gather(packed, 'ctx', axis=0, tiled=False)  74.5 us
    pallas_call x1, Pallas kernels, local_attention(): pl.pallas_call(functools.partial(local_kernel, factor, holders), grid=(he...  38.5 us
    all_gather x2, waiting for transfers between devices, shards(): lax.all_gather(q_own[g * group:(g + 1) * group], 'ctx', axis=0, tiled=False)  35.6 us
    pallas_call x2, Pallas kernels, slash_attention(): pl.pallas_call(functools.partial(slash_kernel, factor, heads, length), gr...  18.7 us
    pallas_call x1, Pallas kernels, sum_over_kvh(): pl.pallas_call(spread_kernel, out_shape=jax.ShapeDtypeStruct((size - 1,)...  16.4 us
    unnamed x19, local copies, waits for them, and re-layouts  8.54 us
    slice x1, local copies, waits for them, and re-layouts, shards(): values[g:g + 1]  6.03 us
    dot_general x1, matrix products, shards(): jnp.dot(attended, out_weight, preferred_element_type=jnp.float32)  5.66 us
  transfers between devices with their start and end apart: 3, of which 3 were waited for; matrix products, arithmetic and copies ran while one was open for 15% of the time, Pallas kernels for 7%

profile of v4, /device:TPU:21, one launch (start us, length us, event | category | flops | bytes accessed | tf_op | source)
XLA Modules:
  0.0 254.1 jit_solution(8141577210727683597)
XLA Ops:
  6.5 1.0 copy.48
  7.5 0.8 fusion.37
  8.4 0.7 all-gather.11.cloned.1.call-update
  9.1 0.7 fusion.26
  11.6 1.1 select_reduce_fusion.1
  12.9 5.0 %copy.50 = bf16[8192,2,128]{2,0,1:T(8,128)(2,1)} copy(bf16[8192,2,128]{2,1,0:T(2,128)(2,1)} %param.11) | data formatting | bytes 8388608 | tf_op args[3]
  17.8 2.6 %copy.49 = bf16[8192,2,128]{2,0,1:T(8,128)(2,1)} copy(bf16[8192,2,128]{2,1,0:T(2,128)(2,1)S(1)} %copy-done) | data formatting | bytes 8388608 | tf_op args[4]
  20.4 2.8 %gather_fusion = bf16[16,64,128]{2,1,0:T(8,128)(2,1)S(1)} fusion(bf16[256,64,128]{2,1,0:T(8,128)(2,1)} %bitcast.64, s32[1024]{0:T(1024)S(1)} %pad_clamp_fusion), kind=kCustom, calls=%fused_computation | custom fusion | bytes 524352 | tf_op jit(solution)/shard_map/gather | solution.py:396
  23.2 2.8 %gather_fusion.1 = bf16[16,64,128]{2,1,0:T(8,128)(2,1)S(1)} fusion(bf16[256,64,128]{2,1,0:T(8,128)(2,1)} %bitcast.66, s32[1024]{0:T(1024)S(1)} %pad_clamp_fusion), kind=kCustom, calls=%fused_computation.1 | custom fusion | bytes 524352 | tf_op jit(solution)/shard_map/gather | solution.py:397
  26.1 0.9 pad_maximum_fusion.1
  27.9 0.7 compare_reduce_fusion.1
  28.8 0.8 reshape.361.bias_ref
  30.6 4.7 %select_reduce_fusion = s32[8,16,96]{2,1,0:T(8,128)S(1)} fusion(s32[8,16,96]{2,1,0:T(8,128)S(1)} %get-tuple-element.66, s32[8,16,96]{2,1,0:T(8,128)S(1)} %minimum_add_fusion, s32[8,96]{1,0:T(8,128)S(1)} %convert_reduce_fusion.1, pred[8,16,96]{2,1,0:T(8,128)(4,1)S(1)} %fusion.2), kind=kLoop, calls=%fused_computation.2 | loop fusion | flops 4706304 | bytes 162816 | tf_op jit(solution)/shard_map/reduce_sum | solution.py:356
  38.0 6.0 %fusion.35 = (bf16[1,8192,128]{2,1,0:T(8,128)(2,1)}, bf16[1,8192,128]{2,1,0:T(8,128)(2,1)}, bf16[1,8192,128]{2,1,0:T(8,128)(2,1)}, bf16[1,8192,128]{2,1,0:T(8,128)(2,1)}) fusion(bf16[2,8192,128]{2,1,0:T(8,128)(2,1)} %bitcast.67, bf16[2,8192,128]{2,1,0:T(8,128)(2,1)} %bitcast.65), kind=kLoop, calls=%fused_computation.122 | loop fusion | bytes 16777216 | tf_op jit(solution)/shard_map/slice | solution.py:413
  44.0 3.7 %all-gather.9.cloned.1.call-done = bf16[32,128,128]{2,1,0:T(8,128)(2,1)} async-done(((bf16[4,128,128]{2,1,0:T(8,128)(2,1)}), bf16[32,128,128]{2,1,0:T(8,128)(2,1)}) %all-gather.9.cloned.1.call-update) | async-done | bytes 1048592 | tf_op jit(solution)/shard_map/all_gather | solution.py:386
  47.7 9.3 %shard_map.82 = (bf16[8,4,128,128]{3,2,1,0:T(8,128)(2,1)}, f32[8,1,4,128]{3,2,1,0:T(4,128)}) custom-call(s32[6144]{0:T(1024)} %reshape.362.list_ref, s32[64]{0:T(128)} %reshape.363.count_ref, bf16[8,4,128,128]{3,2,1,0:T(8,128)(2,1)} %bitcast.85, bf16[1,8192,128]{2,1,0:T(8,128)(2,1)} %get-tuple-element.96.k_ref, bf16[1,8192,128]{2,1,0:T(8,128)(2,1)} %get-tuple-element.54.v_ref), custom_call_target="tpu_custom_call" | custom-call | flops 6442450944 | bytes 12582912 | tf_op jit(solution)/shard_map/pallas_call | solution.py:120
  57.0 31.9 %all-gather.11.cloned.1.call-done = bf16[32,128,128]{2,1,0:T(8,128)(2,1)} async-done(((bf16[4,128,128]{2,1,0:T(8,128)(2,1)}), bf16[32,128,128]{2,1,0:T(8,128)(2,1)}) %all-gather.11.cloned.1.call-update) | async-done | bytes 1048592 | tf_op jit(solution)/shard_map/all_gather | solution.py:386
  88.8 9.4 %shard_map.83 = (bf16[8,4,128,128]{3,2,1,0:T(8,128)(2,1)}, f32[8,1,4,128]{3,2,1,0:T(4,128)}) custom-call(s32[6144]{0:T(1024)} %reshape.364.list_ref, s32[64]{0:T(128)} %reshape.365.count_ref, bf16[8,4,128,128]{3,2,1,0:T(8,128)(2,1)} %bitcast.84, bf16[1,8192,128]{2,1,0:T(8,128)(2,1)} %get-tuple-element.95.k_ref, bf16[1,8192,128]{2,1,0:T(8,128)(2,1)} %get-tuple-element.55.v_ref), custom_call_target="tpu_custom_call" | custom-call | flops 6442450944 | bytes 12582912 | tf_op jit(solution)/shard_map/pallas_call | solution.py:120
  98.2 1.3 pad_maximum_fusion.2.l_ref
  99.6 2.8 %pad_maximum_fusion.o_ref = bf16[8,8,128,128]{3,2,1,0:T(8,128)(2,1)} fusion(bf16[8,4,128,128]{3,2,1,0:T(8,128)(2,1)} %get-tuple-element.14, bf16[8,4,128,128]{3,2,1,0:T(8,128)(2,1)S(1)} %copy-done.2), kind=kLoop, calls=%fused_computation.4 | loop fusion | flops 1048576 | bytes 4194304 | tf_op jit(solution)/shard_map/concatenate | solution.py:418
  102.4 74.5 %all-gather.7.cloned.1.call-done = bf16[320,64,128]{2,1,0:T(8,128)(2,1)} async-done(((bf16[40,64,128]{2,1,0:T(8,128)(2,1)}), bf16[320,64,128]{2,1,0:T(8,128)(2,1)}) %all-gather.7.cloned.1.call-update) | async-done | bytes 5242896 | tf_op jit(solution)/shard_map/all_gather | solution.py:401
  177.0 38.5 %shard_map.84 = (f32[8,128,128]{2,1,0:T(8,128)}, f32[8,1,128]{2,1,0:T(1,128)}, bf16[2,8,128,128]{3,2,1,0:T(8,128)(2,1)}, f32[2,2,4,128]{3,2,1,0:T(4,128)}) custom-call(bf16[8,128,128]{2,1,0:T(8,128)(2,1)} %bitcast.71, bf16[8,40,64,128]{3,2,1,0:T(8,128)(2,1)} %bitcast.60, bf16[8,40,64,128]{3,2,1,0:T(8,128)(2,1)} %bitcast.61, ...), custom_call_target="tpu_custom_call" | custom-call | tf_op jit(solution)/shard_map/pallas_call | solution.py:259
  215.4 0.7 reduce_max.11
  216.8 0.7 exponential_reduce_fusion
  218.2 0.7 fusion.22
  218.9 0.7 exponential_divide_fusion
  219.7 1.4 multiply_reduce_fusion
  221.1 1.2 fusion.1
  222.5 5.7 %convolution_convert_fusion = bf16[128,4096]{1,0:T(8,128)(2,1)} fusion(bf16[128,1024]{0,1:T(8,128)(2,1)S(1)} %bitcast.72, bf16[1024,4096]{1,0:T(8,128)(2,1)} %param.15), kind=kOutput, calls=%fused_computation.3 | convolution fusion | flops 1074266112 | bytes 9699328 | tf_op jit(solution)/shard_map/dot_general | solution.py:446
  228.2 16.4 %shard_map.85 = bf16[3,32,4096]{2,1,0:T(8,128)(2,1)} custom-call(bf16[4,32,4096]{2,1,0:T(8,128)(2,1)} %bitcast.68), custom_call_target="tpu_custom_call" | custom-call | tf_op jit(solution)/shard_map/pallas_call | solution.py:329
  244.6 1.3 convert_reduce_fusion
  245.9 1.7 fusion
  (82 shorter events, 8.2 us)
Async XLA Ops:
  6.5 41.2 %all-gather.9.cloned.1.call-start = ((), (), s32[]{:S(2)}) async-start(), calls=%async_computation.1 | async-start | bytes 1179648 | tf_op jit(solution)/shard_map/all_gather | solution.py:386
  7.5 10.3 %copy-start.1 = (bf16[128,8,128]{2,0,1:T(8,128)(2,1)}, bf16[128,8,128]{2,0,1:T(8,128)(2,1)S(1)}, u32[]{:S(2)}) copy-start(bf16[128,8,128]{2,0,1:T(8,128)(2,1)S(1)} %copy.48) | copy-start | bytes 786436
  8.3 80.5 %all-gather.11.cloned.1.call-start = ((), (), s32[]{:S(2)}) async-start(), calls=%async_computation.2 | async-start | bytes 1179648 | tf_op jit(solution)/shard_map/all_gather | solution.py:386
  9.1 167.9 %all-gather.7.cloned.1.call-start = ((), (), s32[]{:S(2)}) async-start(), calls=%async_computation | async-start | bytes 5898240 | tf_op jit(solution)/shard_map/all_gather | solution.py:401
  12.9 5.0 %copy-start = (bf16[8192,2,128]{2,1,0:T(2,128)(2,1)S(1)}, bf16[8192,2,128]{2,1,0:T(2,128)(2,1)}, u32[]{:S(2)}) copy-start(bf16[8192,2,128]{2,1,0:T(2,128)(2,1)} %param.12) | copy-start | bytes 12582916
  17.8 8.2 %copy-start.4 = (bf16[128,2,128]{2,1,0:T(2,128)(2,1)S(1)}, bf16[128,2,128]{2,1,0:T(2,128)(2,1)}, u32[]{:S(2)}) copy-start(bf16[128,2,128]{2,1,0:T(2,128)(2,1)} %param.9) | copy-start | bytes 196612
  17.8 8.2 %copy-start.5 = (bf16[128,2,128]{2,1,0:T(2,128)(2,1)S(1)}, bf16[128,2,128]{2,1,0:T(2,128)(2,1)}, u32[]{:S(2)}) copy-start(bf16[128,2,128]{2,1,0:T(2,128)(2,1)} %param.10) | copy-start | bytes 196612
  17.8 10.0 %copy-start.3 = (s32[8,96]{1,0:T(8,128)S(1)}, s32[8,96]{1,0:T(8,128)}, u32[]{:S(2)}) copy-start(s32[8,96]{1,0:T(8,128)} %param.14) | copy-start | bytes 9220
  88.8 9.4 %copy-start.6 = (f32[8,1,4,128]{3,2,1,0:T(4,128)S(1)}, f32[8,1,4,128]{3,2,1,0:T(4,128)}, u32[]{:S(2)}) copy-start(f32[8,1,4,128]{3,2,1,0:T(4,128)} %get-tuple-element.15) | copy-start | bytes 49156
  88.8 10.7 %copy-start.2 = (bf16[8,4,128,128]{3,2,1,0:T(8,128)(2,1)S(1)}, bf16[8,4,128,128]{3,2,1,0:T(8,128)(2,1)}, u32[]{:S(2)}) copy-start(bf16[8,4,128,128]{3,2,1,0:T(8,128)(2,1)} %get-tuple-element.13) | copy-start | bytes 3145732
Sparse Core Ops, SparseCore 0:
  9.5 38.1 all-gather.8
  49.8 38.9 all-gather.10
  91.0 85.8 all-gather.6
